TPU v7x, 256 devices: a whole 4x4x8 slice. The times are simulated.
256 devices in a mesh: chan: 32 (over x, y, core), tile: 8 (over z).
Axes of the slice: x: 4, y: 4, z: 8, core: 2. Of those that a mesh axis runs over, the one named last changes fastest.
Arguments:
- amp: bfloat16 [64, 2048, 768], P('chan', 'tile'), may hold values from -6 to 6
- v_pphh: bfloat16 [64, 2048, 768], P('chan', 'tile'), may hold values from -6 to 6
- v_pp: bfloat16 [64, 2048, 2048], P('chan', 'tile'), may hold values from -0.125 to 0.125
- w_ph: bfloat16 [64, 2048, 2048], P('chan', 'tile'), may hold values from -0.125 to 0.125
- coef: bfloat16 [64, 128], P('chan', 'tile'), may hold values from -1 to 1
- target: int32 [64, 128], P('chan', 'tile'), may hold values from 0 to 8191, as said below
- pp_size: int32 [64], P('chan'), may hold values from 16 to 2048
- e_part: float32 [64, 2048], P('chan', 'tile'), may hold values from 0.5 to 4
- e_hole: float32 [64, 768], P('chan'), may hold values from 0.5 to 4
Outputs:
- new_amp: bfloat16 [64, 2048, 768], P('chan', 'tile')
Inputs may be any that keep to these rules, and one draw needn't show every extreme that they name: target is a one-to-one map of all row blocks onto all row blocks; block b goes to a block b2 with b2 // 16 == b // 16; for each value of b // 16, the channels of each group of 2 consecutive channels send exactly 2 * 16 // 32 blocks into each group of 2 consecutive channels.
All inputs are finite; a program needn't handle non-finite values.
Results may differ from a plain program's by a relative error of at most 0.002.
Values may be sent and summed in bfloat16 or wider, within the bound.
No kernel may reach another device: no remote copies, remote signals or barrier semaphores. Data moves between devices by JAX's collectives and lax.ppermute only.
A program may use at most 64 MiB of HBM per device.

v0:
```python
import jax
import jax.numpy as jnp
from jax import lax
from jax.sharding import PartitionSpec as P


def shortened(array):
    return jax.tree.map(lambda a: a.astype(jnp.bfloat16) if a.dtype == jnp.float32 else a, array)


def body(amp, v_pphh, v_pp, w_ph, coef, target, pp_size, e_part, e_hole):
    ch_dev, tile_rows, width = amp.shape
    nb_tile = target.shape[1]
    rows = tile_rows // nb_tile
    n_chan = lax.axis_size("chan")
    n_tile = lax.axis_size("tile")
    blocks = nb_tile * n_tile
    count = ch_dev * nb_tile
    per_peer = count // n_chan
    tile_at = lax.axis_index("tile")
    flat_target = target.reshape(-1)
    flat_coef = coef.reshape(-1).astype(jnp.float32)
    owner = flat_target // blocks // ch_dev
    order = jnp.argsort(owner * count + jnp.arange(count, dtype=jnp.int32))
    whole_amp, whole_target, whole_coef = (
        lax.all_gather(amp, "tile", axis=1, tiled=True),
        lax.all_gather(target, "tile", axis=1, tiled=True),
        lax.all_gather(coef, "tile", axis=1, tiled=True),
    )
    ladder = jnp.einsum("crq,cqh->crh", v_pp, whole_amp, preferred_element_type=jnp.float32)
    all_target = whole_target.reshape(-1)
    all_coef = whole_coef.reshape(-1).astype(jnp.float32)
    position = jnp.arange(ch_dev * blocks, dtype=jnp.int32)
    chan_local = position // blocks
    block_idx = position % blocks
    all_owner = all_target // blocks // ch_dev
    key_sort = (
        all_owner * (n_tile * count)
        + block_idx // nb_tile * count
        + chan_local * nb_tile
        + block_idx % nb_tile
    )
    all_order = jnp.argsort(key_sort)
    full_slot = all_target // blocks % ch_dev * blocks + all_target % blocks
    all_items = (
        whole_amp.reshape(ch_dev * blocks, rows, width).astype(jnp.float32)
        * all_coef[:, None, None]
    ).astype(jnp.bfloat16)
    arrived, arrived_slots = (
        lax.all_to_all(all_items[all_order], "chan", split_axis=0, concat_axis=0, tiled=True),
        lax.all_to_all(
            shortened(full_slot[all_order]), "chan", split_axis=0, concat_axis=0, tiled=True
        ),
    )
    placed = arrived[jnp.argsort(arrived_slots)].reshape(ch_dev, blocks * rows, width)
    cycle = jnp.einsum("crq,cqh->crh", w_ph, placed, preferred_element_type=jnp.float32)
    mine = lax.dynamic_index_in_dim(
        arrived_slots.reshape(n_chan, n_tile, per_peer), tile_at, 1, keepdims=False
    ).reshape(-1)
    back_slots = mine // blocks * nb_tile + mine % blocks % nb_tile
    cycle_items = cycle.astype(jnp.bfloat16).reshape(count, rows, width)
    returned = lax.all_to_all(
        cycle_items[back_slots], "chan", split_axis=0, concat_axis=0, tiled=True
    )
    restored = returned[jnp.argsort(order)].astype(jnp.float32)
    cycle_term = (flat_coef[:, None, None] * restored).reshape(ch_dev, tile_rows, width)
    total = v_pphh.astype(jnp.float32) + ladder + cycle_term
    denom = e_part[:, :, None] + e_hole[:, None, :]
    row_index = tile_at * tile_rows + jnp.arange(tile_rows, dtype=jnp.int32)
    live = row_index[None, :] < pp_size[:, None]
    return jnp.where(live[:, :, None], total / denom, jnp.float32(0.0)).astype(jnp.bfloat16)


def solution(mesh):
    placed = (
        P("chan", "tile", None),
        P("chan", "tile", None),
        P("chan", "tile", None),
        P("chan", "tile", None),
        P("chan", "tile"),
        P("chan", "tile"),
        P("chan"),
        P("chan", "tile"),
        P("chan", None),
    )
    return jax.shard_map(
        body, mesh=mesh, in_specs=placed, out_specs=P("chan", "tile", None), check_vma=False
    )
```

profile of v0, /device:TPU:1, one launch (start us, length us, event | category | flops | bytes accessed | tf_op | source)
XLA Modules:
  0.0 242.2 jit_solution(2513093249997671379)
XLA Ops:
  6.5 0.7 all-gather.4.cloned.1.call-update
  7.3 16.7 %all-gather.1 = s32[8,16,2]{1,2,0:T(2,128)S(1)} all-gather(s32[1,16,2]{1,2,0:T(2,128)} %bitcast.73), channel_id=1, replica_groups=mesh['chan'=32,'tile'=8] {'tile'}, dimensions={0}, use_global_device_ids=true | all-gather | bytes 1152 | tf_op jit(solution)/shard_map/all_gather | solution.py:27
  24.0 0.1 reshape.278
  24.1 3.2 %sort.62 = (s32[256]{0:T(256)}, s32[256]{0:T(256)S(1)}) sort(s32[256]{0:T(256)S(1)} %fusion.7, s32[256]{0:T(256)S(1)} %iota.32), dimensions={0}, to_apply=%region_0.1 | sort | flops 2048 | bytes 4096 | tf_op jit(solution)/shard_map/jit(argsort)/sort | solution.py:43
  27.3 1.9 gather_fusion.1
  29.2 0.7 all_to_all.15
  29.9 11.3 %all-to-all-start.1 = ((s32[32,8,1]{1,2,0:T(1,128)}), s32[32,8,1]{1,2,0:T(1,128)S(1)}, u32[]{:S(2)}, u32[]{:S(2)}) async-start(s32[32,8,1]{1,2,0:T(1,128)} %bitcast.10), calls=%async_computation.1 | async-start | bytes 32768 | tf_op jit(solution)/shard_map/all_to_all | solution.py:51
  41.2 11.6 %all-gather = bf16[8,16,2]{1,2,0:T(2,128)(2,1)S(1)} all-gather(bf16[1,16,2]{1,2,0:T(2,128)(2,1)} %bitcast.72), channel_id=1, replica_groups=mesh['chan'=32,'tile'=8] {'tile'}, dimensions={0}, use_global_device_ids=true | all-gather | bytes 576 | tf_op jit(solution)/shard_map/all_gather | solution.py:28
  52.8 0.1 reshape.279
  52.9 34.7 %all-gather.4.cloned.1.call-done = bf16[2,2048,768]{2,1,0:T(8,128)(2,1)} async-done(((bf16[2,256,768]{2,1,0:T(8,128)(2,1)}), bf16[2,2048,768]{2,1,0:T(8,128)(2,1)}) %all-gather.4.cloned.1.call-update) | async-done | bytes 6291472 | tf_op jit(solution)/shard_map/all_gather | solution.py:26
  87.5 6.5 %fusion = bf16[256,16,768]{2,1,0:T(8,128)(2,1)} fusion(bf16[256,16,768]{2,1,0:T(8,128)(2,1)} %bitcast.67, f32[256]{0:T(256)S(1)} %bitcast.71), kind=kLoop, calls=%fused_computation.6 | loop fusion | flops 9437184 | bytes 12583936 | tf_op jit(solution)/shard_map/convert_element_type | solution.py:48
  94.0 6.4 %gather_fusion = bf16[256,16,768]{2,1,0:T(8,128)(2,1)} fusion(bf16[256,16,768]{2,1,0:T(8,128)(2,1)} %fusion, s32[1024]{0:T(1024)S(1)} %pad_clamp_fusion.3), kind=kCustom, calls=%fused_computation | custom fusion | bytes 12583936 | tf_op jit(solution)/shard_map/gather | solution.py:50
  100.4 7.7 %all-to-all-start = ((bf16[256,16,768]{2,1,0:T(8,128)(2,1)}), bf16[256,16,768]{2,1,0:T(8,128)(2,1)}, u32[]{:S(2)}, u32[]{:S(2)}) async-start(bf16[256,16,768]{2,1,0:T(8,128)(2,1)} %gather_fusion), calls=%async_computation | async-start | bytes 12582912 | tf_op jit(solution)/shard_map/all_to_all | solution.py:50
  108.1 0.1 reshape.227
  108.2 0.5 broadcast.303
  108.7 0.7 reduce.5
  109.4 0.1 all_to_all.17
  109.5 3.2 %sort.63 = (s32[256]{0:T(256)}, s32[256]{0:T(256)S(1)}) sort(s32[256]{0:T(256)S(1)} %all_to_all.17, s32[256]{0:T(256)S(1)} %iota.33), dimensions={0}, to_apply=%region_1.2 | sort | flops 2048 | bytes 4096 | tf_op jit(solution)/shard_map/jit(argsort)/sort | solution.py:55
  112.7 0.7 dynamic-slice_reduce_fusion
  113.5 72.6 %all-to-all-done = bf16[256,16,768]{2,1,0:T(8,128)(2,1)} async-done(((bf16[256,16,768]{2,1,0:T(8,128)(2,1)}), bf16[256,16,768]{2,1,0:T(8,128)(2,1)}, u32[]{:S(2)}, u32[]{:S(2)}) %all-to-all-start) | async-done | bytes 6291488 | tf_op jit(solution)/shard_map/all_to_all | solution.py:50
  186.1 6.4 %gather_fusion.2 = bf16[256,16,768]{2,1,0:T(8,128)(2,1)} fusion(bf16[256,16,768]{2,1,0:T(8,128)(2,1)} %all-to-all-done, s32[1024]{0:T(1024)S(1)} %pad_clamp_fusion.2), kind=kCustom, calls=%fused_computation.2 | custom fusion | bytes 12583936 | tf_op jit(solution)/shard_map/gather | solution.py:55
  192.5 4.6 %convolution_convert_fusion = bf16[2,768,256]{1,2,0:T(8,128)(2,1)S(1)} fusion(bf16[2,256,2048]{2,1,0:T(8,128)(2,1)S(1)} %copy-done, bf16[2,2048,768]{2,1,0:T(8,128)(2,1)} %bitcast.68), kind=kOutput, calls=%fused_computation.12 | convolution fusion | flops 1611005952 | bytes 9175040 | tf_op jit(solution)/shard_map/crq,cqh->crh/dot_general | solution.py:56
  197.1 1.5 gather_fusion.3
  198.6 14.5 %all-to-all-start.2 = ((bf16[32,16,768]{2,1,0:T(8,128)(2,1)}), bf16[32,16,768]{2,1,0:T(8,128)(2,1)S(1)}, u32[]{:S(2)}, u32[]{:S(2)}) async-start(bf16[32,16,768]{2,1,0:T(8,128)(2,1)} %gather_fusion.3), calls=%async_computation.2 | async-start | bytes 1572864 | tf_op jit(solution)/shard_map/all_to_all | solution.py:62
  213.1 0.1 mul.58
  213.2 0.1 mul.59
  213.3 1.6 sort.64
  214.9 1.6 sort.65
  216.6 0.1 broadcast_compare_fusion
  216.6 10.7 %all-to-all-done.2 = bf16[32,16,768]{2,1,0:T(8,128)(2,1)S(1)} async-done(((bf16[32,16,768]{2,1,0:T(8,128)(2,1)}), bf16[32,16,768]{2,1,0:T(8,128)(2,1)S(1)}, u32[]{:S(2)}, u32[]{:S(2)}) %all-to-all-start.2) | async-done | bytes 786464 | tf_op jit(solution)/shard_map/all_to_all | solution.py:62
  227.3 1.5 gather_fusion.4
  228.8 6.5 %fusion.4 = bf16[2,256,768]{2,1,0:T(8,128)(2,1)} fusion(bf16[2,256,768]{2,1,0:T(8,128)(2,1)} %bitcast.69, bf16[2,256,768]{2,1,0:T(8,128)(2,1)} %param.10, bf16[2,256,2048]{2,1,0:T(8,128)(2,1)} %param.11, bf16[2,2048,768]{2,1,0:T(8,128)(2,1)} %all-gather.4.cloned.1.call-done, f32[2,768]{1,0:T(2,128)S(1)} %copy-done.4, f32[2,256]{1,0:T(2,128)S(1)} %copy-done.5, ...), kind=kOutput, calls=%fused_computation.11 | convolution fusion | flops 1614151680 | bytes 10758656 | tf_op jit(solution)/shard_map/crq,cqh->crh/dot_general | solution.py:30
  (32 shorter events, 0.2 us)
Async XLA Ops:
  6.5 185.9 %copy-start = (bf16[2,256,2048]{2,1,0:T(8,128)(2,1)S(1)}, bf16[2,256,2048]{2,1,0:T(8,128)(2,1)}, u32[]{:S(2)}) copy-start(bf16[2,256,2048]{2,1,0:T(8,128)(2,1)} %param.12) | copy-start | bytes 6291460
  6.5 81.0 %all-gather.4.cloned.1.call-start = ((), (), s32[]{:S(2)}) async-start(), calls=%async_computation.3 | async-start | bytes 7077888 | tf_op jit(solution)/shard_map/all_gather | solution.py:26
  29.9 70.5 %all-to-all-start.1 = ((s32[32,8,1]{1,2,0:T(1,128)}), s32[32,8,1]{1,2,0:T(1,128)S(1)}, u32[]{:S(2)}, u32[]{:S(2)}) async-start(s32[32,8,1]{1,2,0:T(1,128)} %bitcast.10), calls=%async_computation.1 | async-start | bytes 32768 | tf_op jit(solution)/shard_map/all_to_all | solution.py:51
  100.4 7.7 %copy-start.2 = (s32[2,16]{1,0:T(2,128)S(1)}, s32[2,16]{1,0:T(2,128)}, u32[]{:S(2)}) copy-start(s32[2,16]{1,0:T(2,128)} %param.14) | copy-start | bytes 388
  100.4 85.7 %all-to-all-start = ((bf16[256,16,768]{2,1,0:T(8,128)(2,1)}), bf16[256,16,768]{2,1,0:T(8,128)(2,1)}, u32[]{:S(2)}, u32[]{:S(2)}) async-start(bf16[256,16,768]{2,1,0:T(8,128)(2,1)} %gather_fusion), calls=%async_computation | async-start | bytes 12582912 | tf_op jit(solution)/shard_map/all_to_all | solution.py:50
  192.4 20.7 %copy-start.1 = (bf16[2,16]{1,0:T(2,128)(2,1)S(1)}, bf16[2,16]{1,0:T(2,128)(2,1)}, u32[]{:S(2)}) copy-start(bf16[2,16]{1,0:T(2,128)(2,1)} %param.13) | copy-start | bytes 196
  192.4 24.1 %copy-start.3 = (s32[2]{0:T(128)S(1)}, s32[2]{0:T(128)}, u32[]{:S(2)}) copy-start(s32[2]{0:T(128)} %param.15) | copy-start | bytes 28
  192.4 36.4 %copy-start.4 = (f32[2,768]{1,0:T(2,128)S(1)}, f32[2,768]{1,0:T(2,128)}, u32[]{:S(2)}) copy-start(f32[2,768]{1,0:T(2,128)} %param.17) | copy-start | bytes 18436
  192.5 36.4 %copy-start.5 = (f32[2,256]{1,0:T(2,128)S(1)}, f32[2,256]{1,0:T(2,128)}, u32[]{:S(2)}) copy-start(f32[2,256]{1,0:T(2,128)} %param.16) | copy-start | bytes 6148
  198.6 28.8 %all-to-all-start.2 = ((bf16[32,16,768]{2,1,0:T(8,128)(2,1)}), bf16[32,16,768]{2,1,0:T(8,128)(2,1)S(1)}, u32[]{:S(2)}, u32[]{:S(2)}) async-start(bf16[32,16,768]{2,1,0:T(8,128)(2,1)} %gather_fusion.3), calls=%async_computation.2 | async-start | bytes 1572864 | tf_op jit(solution)/shard_map/all_to_all | solution.py:62
Sparse Core Ops, SparseCore 0:
  9.2 78.3 all-gather.3
where the time goes:
time: 243 us; the launch traced here: 242 us
  waiting for transfers between devices  119 us (49%)
  starting transfers between devices  33.5 us (14%)
  blocking collectives  28.3 us (12%)
  local copies, waits for them, and re-layouts  20.1 us (8%)
  other arithmetic  17 us (7%)
  between operations  13.6 us (6%)
  matrix products  11.2 us (5%)
    all_to_all x1, waiting for transfers between devices, body(): lax.all_to_all(all_items[all_order], 'chan', split_axis=0, concat_axis=0,...  72.6 us
    all_gather x1, waiting for transfers between devices, body(): lax.all_gather(amp, 'tile', axis=1, tiled=True)  34.7 us
    all_gather x1, blocking collectives, body(): lax.all_gather(target, 'tile', axis=1, tiled=True)  16.7 us
    all_to_all x1, starting transfers between devices, body(): lax.all_to_all(cycle_items[back_slots], 'chan', split_axis=0, concat_axis...  14.5 us
    all_gather x1, blocking collectives, body(): lax.all_gather(coef, 'tile', axis=1, tiled=True)  11.6 us
    all_to_all x1, starting transfers between devices, body(): lax.all_to_all(shortened(full_slot[all_order]), 'chan', split_axis=0, con...  11.3 us
    all_to_all x1, waiting for transfers between devices, body(): lax.all_to_all(cycle_items[back_slots], 'chan', split_axis=0, concat_axis...  10.7 us
    all_to_all x1, starting transfers between devices, body(): lax.all_to_all(all_items[all_order], 'chan', split_axis=0, concat_axis=0,...  7.71 us
  transfers between devices with their start and end apart: 4, of which 3 were waited for; matrix products, arithmetic and copies ran while one was open for 11% of the time, Pallas kernels for 0%

commit v1 on v0

v1 whole, which is shorter than its diff:
```python
import functools

import jax
import jax.numpy as jnp
from jax import lax
from jax.experimental import pallas as pl
from jax.experimental.pallas import tpu as pltpu
from jax.sharding import PartitionSpec as P

META = 128
NEAR = 512
VMEM_LIMIT = 56 * 1024 * 1024

F32, BF16, I32 = jnp.float32, jnp.bfloat16, jnp.int32


def call(kernel, outs, operands, scalars, scratch=(), flops=0, moved=0):
    smem, vmem = pl.BlockSpec(memory_space=pltpu.SMEM), pl.BlockSpec(memory_space=pltpu.VMEM)
    return pl.pallas_call(
        kernel,
        out_shape=outs,
        in_specs=[smem] * len(scalars) + [vmem] * len(operands),
        out_specs=jax.tree.map(lambda _: vmem, outs),
        scratch_shapes=list(scratch),
        compiler_params=pltpu.CompilerParams(vmem_limit_bytes=VMEM_LIMIT),
        cost_estimate=pl.CostEstimate(flops=flops, bytes_accessed=moved, transcendentals=0),
    )(*scalars, *operands)


def pack_kernel(blocks, ch_dev, own, slot, coef, where, amp, items, near):
    count, rows, width = amp.shape
    near_width = near.shape[2]
    lane = lax.broadcasted_iota(I32, (rows, META), 1)
    place = lax.broadcasted_iota(I32, (rows, 2 * META), 0)
    place += rows * (lax.broadcasted_iota(I32, (rows, 2 * META), 1) // META)
    names = jnp.zeros((rows, 2 * META), F32)
    for b in range(count):
        to = own[b]
        block = amp[b]
        items[to, :, :width] = (block.astype(F32) * coef[b]).astype(BF16)
        note = jnp.where(lane < META // 2, slot[b].astype(F32), coef[b])
        items[to, :, width:] = note.astype(BF16)
        near[to] = block[:, :near_width]
        names = jnp.where(place == to, where[b].astype(F32), names)
    near[count] = jnp.zeros((rows, near_width), BF16)
    near[count, :, : 2 * META] = names.astype(BF16)


def settle_kernel(slot, got, far):
    count, rows, wide = got.shape
    width = wide - META
    far_width = far.shape[2]
    row = lax.broadcasted_iota(I32, (rows, META), 0)
    notes = [jnp.zeros((rows, META), BF16)] * 2
    for c in range(count):
        far[slot[c]] = got[c, :, width - far_width : width]
        note = got[c, :, width:].astype(F32)
        kept = notes[c // rows].astype(F32)
        notes[c // rows] = jnp.where(row == c % rows, note, kept).astype(BF16)
    for part in range(2):
        far[count, :, part * META : (part + 1) * META] = notes[part]


def cycle_kernel(tiles, row, coef, home, own, pair_a, pair_b, pair_c, last, *rest):
    far, (w_ph, back, placed, result) = rest[:-4], rest[-4:]
    count, rows, width = back.shape
    near = last.shape[2]
    ch_dev, total, _ = placed.shape
    per = total // len(far)

    def put(piece, c, block):
        at = row[piece * count + c]
        scaled = (block.astype(F32) * coef[piece * count + c]).astype(BF16)
        placed[at // total, pl.ds(pl.multiple_of(at % total, rows), rows), :near] = scaled

    def step(c, carry):
        at = row[c]
        placed[at // total, pl.ds(pl.multiple_of(at % total, rows), rows), :near] = own[c, :, :near]
        for i, pair in enumerate((pair_a, pair_b, pair_c)):
            put(2 * i + 1, c, pair[c, 0])
            put(2 * i + 2, c, pair[c, 1])
        put(7, c, last[c])
        return carry

    lax.fori_loop(0, count, step, 0, unroll=2)
    each = count // ch_dev
    for piece, ref in enumerate(far):
        at = pl.ds(pl.multiple_of(tiles[piece] * per, per), per)
        for ch in range(ch_dev):
            block = ref[ch * each : (ch + 1) * each]
            placed[ch, at, near:] = block.reshape(per, width - near)
    for ch in range(ch_dev):
        result[ch] = jnp.dot(w_ph[ch], placed[ch], preferred_element_type=F32).astype(BF16)
    for c in range(count):
        at = home[c]
        back[c] = result[at // each, pl.ds(pl.multiple_of(at % each * rows, rows), rows), :]


def near_kernel(row, *refs):
    pieces, (v_pp, ladder, placed) = refs[:-3], refs[-3:]
    ch_dev, total, _ = placed.shape
    count, rows = pieces[0].shape[0] - 1, pieces[0].shape[1]

    def step(c, carry):
        for piece, ref in enumerate(pieces):
            at = row[piece * count + c]
            placed[at // total, pl.ds(pl.multiple_of(at % total, rows), rows), :] = ref[c]
        return carry

    lax.fori_loop(0, count, step, 0, unroll=2)
    for ch in range(ch_dev):
        ladder[ch] = jnp.dot(v_pp[ch], placed[ch], preferred_element_type=F32)


def final_kernel(own, live, coef, far, v_pp, ladder, back, v_pphh, e_part, e_hole, out):
    ch_dev, per, width = out.shape
    count, rows, _ = back.shape
    near = ladder.shape[2]
    each = count // ch_dev
    for ch in range(ch_dev):
        more = jnp.dot(v_pp[ch], far[ch], preferred_element_type=F32)
        for b in range(each):
            i = ch * each + b
            at = slice(b * rows, (b + 1) * rows)
            come = back[own[i]].astype(F32) * coef[i]
            sums = jnp.concatenate([ladder[ch, at], more[at]], axis=1)
            sums = v_pphh[ch, at].astype(F32) + sums + come
            denom = e_part[ch, at] + e_hole[ch]
            row = lax.broadcasted_iota(I32, (rows, width), 0) + b * rows
            out[ch, at] = jnp.where(row < live[ch], sums / denom, 0.0).astype(BF16)


def body(amp, v_pphh, v_pp, w_ph, coef, target, pp_size, e_part, e_hole):
    ch_dev, tile_rows, width = amp.shape
    nb_tile = target.shape[1]
    rows = tile_rows // nb_tile
    n_tile = lax.axis_size("tile")
    blocks = nb_tile * n_tile
    count = ch_dev * nb_tile
    far_width = width - NEAR
    total = tile_rows * n_tile
    me = lax.axis_index("tile")
    right = [(i, (i + 1) % n_tile) for i in range(n_tile)]
    left = [((i + 1) % n_tile, i) for i in range(n_tile)]
    to_right = functools.partial(lax.ppermute, axis_name="tile", perm=right)
    to_left = functools.partial(lax.ppermute, axis_name="tile", perm=left)
    exchange = functools.partial(
        lax.all_to_all, axis_name="chan", split_axis=0, concat_axis=0, tiled=True
    )

    flat_target = target.reshape(-1)
    flat_coef = coef.reshape(-1).astype(F32)
    own = flat_target // (ch_dev * blocks)
    slot = flat_target % (ch_dev * blocks)
    index = jnp.arange(count, dtype=I32)
    where = index // nb_tile * blocks + me * nb_tile + index % nb_tile

    def row_of(names):
        return names // blocks * total + names % blocks * rows

    items, near = call(
        functools.partial(pack_kernel, blocks, ch_dev),
        (
            jax.ShapeDtypeStruct((count, rows, width + META), BF16),
            jax.ShapeDtypeStruct((count + 1, rows, NEAR), BF16),
        ),
        (amp.reshape(count, rows, width),),
        (own, slot, flat_coef, where),
    )
    r1, l1 = to_right(near), to_left(near)
    got = exchange(items)
    got_slot = got[:, 0, width].astype(I32)
    home = got_slot // blocks * nb_tile + got_slot % nb_tile
    far = call(
        settle_kernel,
        jax.ShapeDtypeStruct((count + 1, rows, far_width), BF16),
        (got,),
        (home,),
    )
    fr1, fl1 = to_right(far), to_left(far)
    r2, l2 = to_right(r1), to_left(l1)
    fr2, fl2 = to_right(fr1), to_left(fl1)
    r3, l3 = to_right(r2), to_left(l2)
    fr3, fl3 = to_right(fr2), to_left(fl2)
    r4 = to_right(r3)
    fl4 = to_left(fl3)

    def pair(a, b):
        return exchange(jnp.stack([a[:count], b[:count]], axis=1))

    got_a, got_b, got_c = pair(r1, l1), pair(r2, l2), pair(r3, l3)
    got_d = exchange(r4[:count])

    near_all = (near, r1, l1, r2, l2, r3, l3, r4)
    far_all = (far, fr1, fl1, fr2, fl2, fr3, fl3, fl4)
    steps = jnp.array([0, -1, 1, -2, 2, -3, 3, 4], dtype=I32)
    tiles = (me + steps + n_tile) % n_tile

    def notes(pieces, lane):
        kept = jnp.stack([p[count, :, : 2 * META] for p in pieces])
        kept = kept.reshape(len(pieces), rows, 2, META)[:, :, :, lane]
        return kept.transpose(0, 2, 1).reshape(-1)

    back = call(
        cycle_kernel,
        jax.ShapeDtypeStruct((count, rows, width), BF16),
        (got, got_a, got_b, got_c, got_d, *far_all, w_ph),
        (
            tiles,
            row_of(notes(far_all, 0).astype(I32)),
            notes(far_all, META // 2).astype(F32),
            home,
        ),
        scratch=(
            pltpu.VMEM((ch_dev, total, width), BF16),
            pltpu.VMEM((ch_dev, tile_rows, width), BF16),
        ),
        flops=2 * ch_dev * tile_rows * total * width,
        moved=20 * 2**20,
    )
    returned = exchange(back)

    ladder = call(
        near_kernel,
        jax.ShapeDtypeStruct((ch_dev, tile_rows, NEAR), F32),
        (*near_all, v_pp),
        (row_of(notes(near_all, 0).astype(I32)),),
        scratch=(pltpu.VMEM((ch_dev, total, NEAR), BF16),),
        flops=2 * ch_dev * tile_rows * total * NEAR,
        moved=10 * 2**20,
    )
    whole_far = lax.all_gather(amp[:, :, NEAR:], "tile", axis=1, tiled=True)
    return call(
        final_kernel,
        jax.ShapeDtypeStruct((ch_dev, tile_rows, width), BF16),
        (
            whole_far,
            v_pp,
            ladder,
            returned,
            v_pphh,
            e_part[:, :, None],
            e_hole[:, None, :],
        ),
        (own, pp_size - me * tile_rows, flat_coef),
        flops=2 * ch_dev * tile_rows * total * far_width,
        moved=10 * 2**20,
    )


def solution(mesh):
    placed = (
        P("chan", "tile", None),
        P("chan", "tile", None),
        P("chan", "tile", None),
        P("chan", "tile", None),
        P("chan", "tile"),
        P("chan", "tile"),
        P("chan"),
        P("chan", "tile"),
        P("chan", None),
    )
    return jax.shard_map(
        body, mesh=mesh, in_specs=placed, out_specs=P("chan", "tile", None), check_vma=False
    )
```

time: 243 us -> 183 us (0.75)
  waiting for transfers between devices: 119 us -> 53.7 us
  blocking collectives: 28.3 us -> 0 us
  starting transfers between devices: 33.5 us -> 59.4 us
  Pallas kernels: 0 us -> 25.5 us
  other arithmetic: 17 us -> 5.03 us
  matrix products: 11.2 us -> 0 us
  local copies, waits for them, and re-layouts: 20.1 us -> 23.9 us
    all_to_all x3 -> x6, waiting for transfers between devices: 83.3 us -> 28 us  [the longest x1 9.98 us: body(): got_d = exchange(r4[:count])]
    all_gather x1, waiting for transfers between devices: 34.7 us -> 0.01 us  [body(): whole_far = lax.all_gather(amp[:, :, NEAR:], 'tile', axis=1, tiled=True)]
    all_gather x2 -> x0, blocking collectives: 28.3 us -> none  [the longest x1 16.7 us: body(): lax.all_gather(target, 'tile', axis=1, tiled=True)]
    ppermute x0 -> x14, waiting for transfers between devices: none -> 25.7 us  [the longest x1 9.59 us: body(): r4 = to_right(r3)]
    pallas_call x0 -> x5, Pallas kernels: none -> 25.5 us  [call(): pl.pallas_call(kernel, out_shape=outs, in_specs=[smem] * len(scalars) + [...]
    ppermute x0 -> x14, starting transfers between devices: none -> 22.5 us  [the longest x2 6.41 us: body(): r1, l1 = (to_right(near), to_left(near))]
    gather x5 -> x0, local copies, waits for them, and re-layouts: 17.6 us -> none  [the longest x1 6.35 us: body(): arrived[jnp.argsort(arrived_slots)].reshape(ch_dev, blocks * rows, width)]
    dot_general x2 -> x0, matrix products: 11.2 us -> none  [the longest x1 6.55 us: body(): jnp.einsum('crq,cqh->crh', v_pp, whole_amp, preferred_element_type=jnp.fl...]
  transfers between devices with their start and end apart: 4 -> 21, of which waited for: 3 -> 9; matrix products, arithmetic and copies ran while one was open for 11% -> 13% of each run, Pallas kernels for 0% -> 10%
where the time goes in v1:
time: 183 us; the launch traced here: 181 us
  starting transfers between devices  59.4 us (32%)
  waiting for transfers between devices  53.7 us (29%)
  Pallas kernels  25.5 us (14%)
  local copies, waits for them, and re-layouts  23.9 us (13%)
  between operations  13.7 us (7%)
  other arithmetic  5.03 us (3%)
    pallas_call x5, Pallas kernels, call(): pl.pallas_call(kernel, out_shape=outs, in_specs=[smem] * len(scalars) + [...  25.5 us
    all_to_all x3, starting transfers between devices, pair(): return exchange(jnp.stack([a[:count], b[:count]], axis=1))  17.1 us
    unnamed x52, local copies, waits for them, and re-layouts  10 us
    all_to_all x1, waiting for transfers between devices, body(): got_d = exchange(r4[:count])  9.98 us
    ppermute x1, waiting for transfers between devices, body(): r4 = to_right(r3)  9.59 us
    all_to_all x1, waiting for transfers between devices, body(): got = exchange(items)  8.12 us
    all_to_all x1, starting transfers between devices, body(): got_d = exchange(r4[:count])  8.08 us
    all_to_all x1, starting transfers between devices, body(): got = exchange(items)  8.05 us
  transfers between devices with their start and end apart: 21, of which 9 were waited for; matrix products, arithmetic and copies ran while one was open for 13% of the time, Pallas kernels for 10%

profile of v1, /device:TPU:1, one launch (start us, length us, event | category | flops | bytes accessed | tf_op | source)
XLA Modules:
  0.0 181.2 jit_solution(13414325506424911731)
XLA Ops:
  7.9 1.3 reshape.37.coef
  9.9 2.5 %shard_map.100 = (bf16[32,16,896]{2,1,0:T(8,128)(2,1)}, bf16[33,16,512]{2,1,0:T(8,128)(2,1)}) custom-call(s32[32]{0:T(128)} %get-tuple-element.12.own, s32[32]{0:T(128)} %get-tuple-element.11.slot, f32[32]{0:T(128)} %reshape.37.coef, s32[32]{0:T(128)} %fusion.5.where, bf16[32,16,768]{2,1,0:T(8,128)(2,1)} %bitcast.37), custom_call_target="tpu_custom_call" | custom-call | tf_op jit(solution)/shard_map/pallas_call | solution.py:19
  12.4 2.5 %collective-permute-start = (bf16[33,16,512]{2,1,0:T(8,128)(2,1)}, bf16[33,16,512]{2,1,0:T(8,128)(2,1)S(1)}, u32[]{:S(2)}, u32[]{:S(2)}) collective-permute-start(bf16[33,16,512]{2,1,0:T(8,128)(2,1)} %get-tuple-element.7.refs_0_), channel_id=1, source_target_pairs={{0,1},{1,2},{2,3},{3,4},{4,5},{5,6},{6,7},{7,0},{8,9},{9,10},{10,1... | collective-permute-start | bytes 1622024 | tf_op jit(solution)/shard_map/ppermute | solution.py:170
  14.9 3.9 %collective-permute-start.1 = (bf16[33,16,512]{2,1,0:T(8,128)(2,1)}, bf16[33,16,512]{2,1,0:T(8,128)(2,1)S(1)}, u32[]{:S(2)}, u32[]{:S(2)}) collective-permute-start(bf16[33,16,512]{2,1,0:T(8,128)(2,1)} %get-tuple-element.7.refs_0_), channel_id=1, source_target_pairs={{1,0},{2,1},{3,2},{4,3},{5,4},{6,5},{7,6},{0,7},{9,8},{10,9},{11,1... | collective-permute-start | bytes 1622024 | tf_op jit(solution)/shard_map/ppermute | solution.py:170
  18.8 1.7 slice.92
  20.5 8.1 %all-to-all-start = ((bf16[32,16,896]{2,1,0:T(8,128)(2,1)}), bf16[32,16,896]{2,1,0:T(8,128)(2,1)S(1)}, u32[]{:S(2)}, u32[]{:S(2)}) async-start(bf16[32,16,896]{2,1,0:T(8,128)(2,1)} %get-tuple-element.8), calls=%async_computation | async-start | bytes 1835008 | tf_op jit(solution)/shard_map/all_to_all | solution.py:171
  32.1 1.1 copy.30
  33.2 2.7 %collective-permute-start.3 = (bf16[33,16,512]{2,1,0:T(8,128)(2,1)S(1)}, bf16[33,16,512]{2,1,0:T(8,128)(2,1)}, u32[]{:S(2)}, u32[]{:S(2)}) collective-permute-start(bf16[33,16,512]{2,1,0:T(8,128)(2,1)S(1)} %collective-permute-done.1.refs_2_), channel_id=1, source_target_pairs={{1,0},{2,1},{3,2},{4,3},{5,4},{6,5},{7,6},{0,7},{9,8},{10,9},{11,1... | collective-permute-start | bytes 1622024 | tf_op jit(solution)/shard_map/ppermute | solution.py:181
  35.9 8.1 %all-to-all-done.got.own = bf16[32,16,896]{2,1,0:T(8,128)(2,1)S(1)} async-done(((bf16[32,16,896]{2,1,0:T(8,128)(2,1)}), bf16[32,16,896]{2,1,0:T(8,128)(2,1)S(1)}, u32[]{:S(2)}, u32[]{:S(2)}) %all-to-all-start) | async-done | bytes 917536 | tf_op jit(solution)/shard_map/all_to_all | solution.py:171
  44.0 4.0 %all-to-all-start.1 = ((bf16[32,2,16,512]{3,2,1,0:T(8,128)(2,1)}), bf16[32,2,16,512]{3,2,1,0:T(8,128)(2,1)S(1)}, u32[]{:S(2)}, u32[]{:S(2)}) async-start(bf16[32,2,16,512]{3,2,1,0:T(8,128)(2,1)} %copy.30), calls=%async_computation.1 | async-start | bytes 2097152 | tf_op jit(solution)/shard_map/all_to_all | solution.py:189
  49.3 1.9 %shard_map.102.rest_0_ = bf16[33,16,256]{2,1,0:T(8,128)(2,1)} custom-call(s32[32]{0:T(128)} %fusion.6.slot.home, bf16[32,16,896]{2,1,0:T(8,128)(2,1)} %copy-done), custom_call_target="tpu_custom_call" | custom-call | tf_op jit(solution)/shard_map/pallas_call | solution.py:19
  51.2 2.7 %collective-permute-start.8 = (bf16[33,16,256]{2,1,0:T(8,128)(2,1)}, bf16[33,16,256]{2,1,0:T(8,128)(2,1)}, u32[]{:S(2)}, u32[]{:S(2)}) collective-permute-start(bf16[33,16,256]{2,1,0:T(8,128)(2,1)} %shard_map.102.rest_0_), channel_id=1, source_target_pairs={{1,0},{2,1},{3,2},{4,3},{5,4},{6,5},{7,6},{0,7},{9,8},{10,9},{11,1... | collective-permute-start | bytes 811016 | tf_op jit(solution)/shard_map/ppermute | solution.py:180
  54.6 3.7 %collective-permute-done.3.refs_4_ = bf16[33,16,512]{2,1,0:T(8,128)(2,1)} collective-permute-done((bf16[33,16,512]{2,1,0:T(8,128)(2,1)S(1)}, bf16[33,16,512]{2,1,0:T(8,128)(2,1)}, u32[]{:S(2)}, u32[]{:S(2)}) %collective-permute-start.3) | collective-permute-done | bytes 540704 | tf_op jit(solution)/shard_map/ppermute | solution.py:181
  59.8 1.1 slice_bitcast_fusion.3
  62.5 2.2 %collective-permute-start.5 = (bf16[33,16,512]{2,1,0:T(8,128)(2,1)}, bf16[33,16,512]{2,1,0:T(8,128)(2,1)S(1)}, u32[]{:S(2)}, u32[]{:S(2)}) collective-permute-start(bf16[33,16,512]{2,1,0:T(8,128)(2,1)} %collective-permute-done.3.refs_4_), channel_id=1, source_target_pairs={{1,0},{2,1},{3,2},{4,3},{5,4},{6,5},{7,6},{0,7},{9,8},{10,9},{11,1... | collective-permute-start | bytes 1622024 | tf_op jit(solution)/shard_map/ppermute | solution.py:183
  66.1 5.2 %collective-permute-done.7.rest_1_ = bf16[33,16,256]{2,1,0:T(8,128)(2,1)S(1)} collective-permute-done((bf16[33,16,256]{2,1,0:T(8,128)(2,1)}, bf16[33,16,256]{2,1,0:T(8,128)(2,1)S(1)}, u32[]{:S(2)}, u32[]{:S(2)}) %collective-permute-start.7) | collective-permute-done | bytes 270368 | tf_op jit(solution)/shard_map/ppermute | solution.py:180
  71.4 2.7 %collective-permute-start.10 = (bf16[33,16,256]{2,1,0:T(8,128)(2,1)}, bf16[33,16,256]{2,1,0:T(8,128)(2,1)}, u32[]{:S(2)}, u32[]{:S(2)}) collective-permute-start(bf16[33,16,256]{2,1,0:T(8,128)(2,1)} %collective-permute-done.8.rest_2_), channel_id=1, source_target_pairs={{1,0},{2,1},{3,2},{4,3},{5,4},{6,5},{7,6},{0,7},{9,8},{10,9},{11,1... | collective-permute-start | bytes 811016 | tf_op jit(solution)/shard_map/ppermute | solution.py:182
  74.0 9.2 %all-to-all-start.2 = ((bf16[32,2,16,512]{3,2,1,0:T(8,128)(2,1)}), bf16[32,2,16,512]{3,2,1,0:T(8,128)(2,1)S(1)}, u32[]{:S(2)}, u32[]{:S(2)}) async-start(bf16[32,2,16,512]{3,2,1,0:T(8,128)(2,1)} %copy.31), calls=%async_computation.2 | async-start | bytes 2097152 | tf_op jit(solution)/shard_map/all_to_all | solution.py:189
  83.9 6.8 %collective-permute-done.9.rest_3_ = bf16[33,16,256]{2,1,0:T(8,128)(2,1)} collective-permute-done((bf16[33,16,256]{2,1,0:T(8,128)(2,1)S(1)}, bf16[33,16,256]{2,1,0:T(8,128)(2,1)}, u32[]{:S(2)}, u32[]{:S(2)}) %collective-permute-start.9) | collective-permute-done | bytes 270368 | tf_op jit(solution)/shard_map/ppermute | solution.py:182
  90.7 2.7 %collective-permute-start.12 = (bf16[33,16,256]{2,1,0:T(8,128)(2,1)}, bf16[33,16,256]{2,1,0:T(8,128)(2,1)}, u32[]{:S(2)}, u32[]{:S(2)}) collective-permute-start(bf16[33,16,256]{2,1,0:T(8,128)(2,1)} %collective-permute-done.10.rest_4_), channel_id=1, source_target_pairs={{1,0},{2,1},{3,2},{4,3},{5,4},{6,5},{7,6},{0,7},{9,8},{10,9},{11,1... | collective-permute-start | bytes 811016 | tf_op jit(solution)/shard_map/ppermute | solution.py:184
  94.3 1.1 copy.32
  95.4 4.7 %all-to-all-done.2.pair_b = bf16[32,2,16,512]{3,2,1,0:T(8,128)(2,1)S(1)} async-done(((bf16[32,2,16,512]{3,2,1,0:T(8,128)(2,1)}), bf16[32,2,16,512]{3,2,1,0:T(8,128)(2,1)S(1)}, u32[]{:S(2)}, u32[]{:S(2)}) %all-to-all-start.2) | async-done | bytes 1048608 | tf_op jit(solution)/shard_map/all_to_all | solution.py:189
  100.1 4.0 %all-to-all-start.3 = ((bf16[32,2,16,512]{3,2,1,0:T(8,128)(2,1)}), bf16[32,2,16,512]{3,2,1,0:T(8,128)(2,1)S(1)}, u32[]{:S(2)}, u32[]{:S(2)}) async-start(bf16[32,2,16,512]{3,2,1,0:T(8,128)(2,1)} %copy.32), calls=%async_computation.3 | async-start | bytes 2097152 | tf_op jit(solution)/shard_map/all_to_all | solution.py:189
  106.0 2.7 %collective-permute-start.13 = (bf16[33,16,256]{2,1,0:T(8,128)(2,1)}, bf16[33,16,256]{2,1,0:T(8,128)(2,1)S(1)}, u32[]{:S(2)}, u32[]{:S(2)}) collective-permute-start(bf16[33,16,256]{2,1,0:T(8,128)(2,1)} %collective-permute-done.12.rest_6_), channel_id=1, source_target_pairs={{1,0},{2,1},{3,2},{4,3},{5,4},{6,5},{7,6},{0,7},{9,8},{10,9},{11,1... | collective-permute-start | bytes 811016 | tf_op jit(solution)/shard_map/ppermute | solution.py:186
  110.1 9.6 %collective-permute-done.6.refs_7_ = bf16[33,16,512]{2,1,0:T(8,128)(2,1)S(1)} collective-permute-done((bf16[33,16,512]{2,1,0:T(8,128)(2,1)S(1)}, bf16[33,16,512]{2,1,0:T(8,128)(2,1)S(1)}, u32[]{:S(2)}, u32[]{:S(2)}) %collective-permute-start.6) | collective-permute-done | bytes 540704 | tf_op jit(solution)/shard_map/ppermute | solution.py:185
  121.3 8.1 %all-to-all-start.4 = ((bf16[32,16,512]{2,1,0:T(8,128)(2,1)}), bf16[32,16,512]{2,1,0:T(8,128)(2,1)S(1)}, u32[]{:S(2)}, u32[]{:S(2)}) async-start(bf16[32,16,512]{2,1,0:T(8,128)(2,1)} %slice.145), calls=%async_computation.4 | async-start | bytes 1048576 | tf_op jit(solution)/shard_map/all_to_all | solution.py:192
  131.0 10.0 %all-to-all-done.4.last = bf16[32,16,512]{2,1,0:T(8,128)(2,1)S(1)} async-done(((bf16[32,16,512]{2,1,0:T(8,128)(2,1)}), bf16[32,16,512]{2,1,0:T(8,128)(2,1)S(1)}, u32[]{:S(2)}, u32[]{:S(2)}) %all-to-all-start.4) | async-done | bytes 524320 | tf_op jit(solution)/shard_map/all_to_all | solution.py:192
  141.8 8.8 %shard_map.103 = bf16[32,16,768]{2,1,0:T(8,128)(2,1)} custom-call(s32[8]{0:T(128)} %and_select_fusion.4.tiles, s32[256]{0:T(256)} %fusion.4.row, f32[256]{0:T(256)} %reshape.41.coef, s32[32]{0:T(128)} %fusion.6.slot.home, bf16[32,16,896]{2,1,0:T(8,128)(2,1)} %copy-done, bf16[32,2,16,512]{3,2,1,0:T(8,128)(2,1)} %copy-done.1, ...), custom_call_target="tpu_custom_call" | custom-call | flops 1610612736 | bytes 20971520 | tf_op jit(solution)/shard_map/pallas_call | solution.py:19
  150.6 3.7 %all-to-all-start.5 = ((bf16[32,16,768]{2,1,0:T(8,128)(2,1)}), bf16[32,16,768]{2,1,0:T(8,128)(2,1)S(1)}, u32[]{:S(2)}, u32[]{:S(2)}) async-start(bf16[32,16,768]{2,1,0:T(8,128)(2,1)} %shard_map.103), calls=%async_computation.5 | async-start | bytes 1572864 | tf_op jit(solution)/shard_map/all_to_all | solution.py:221
  156.1 7.2 %shard_map.101.ladder = f32[2,256,512]{2,1,0:T(8,128)} custom-call(s32[256]{0:T(256)} %fusion.2.row, bf16[33,16,512]{2,1,0:T(8,128)(2,1)} %get-tuple-element.7.refs_0_, bf16[33,16,512]{2,1,0:T(8,128)(2,1)} %copy-done.5, bf16[33,16,512]{2,1,0:T(8,128)(2,1)} %copy-done.6, bf16[33,16,512]{2,1,0:T(8,128)(2,1)} %collective-permute-done.2.refs_3_, ...), custom_call_target="tpu_custom_call" | custom-call | flops 1073741824 | bytes 10485760 | tf_op jit(solution)/shard_map/pallas_call | solution.py:19
  163.3 5.2 %all-to-all-done.5.back = bf16[32,16,768]{2,1,0:T(8,128)(2,1)S(1)} async-done(((bf16[32,16,768]{2,1,0:T(8,128)(2,1)}), bf16[32,16,768]{2,1,0:T(8,128)(2,1)S(1)}, u32[]{:S(2)}, u32[]{:S(2)}) %all-to-all-start.5) | async-done | bytes 786464 | tf_op jit(solution)/shard_map/all_to_all | solution.py:221
  169.4 5.0 %shard_map.104 = bf16[2,256,768]{2,1,0:T(8,128)(2,1)} custom-call(s32[32]{0:T(128)} %get-tuple-element.12.own, s32[2]{0:T(128)} %broadcast_subtract_fusion.live, f32[32]{0:T(128)} %reshape.37.coef, bf16[2,2048,256]{2,1,0:T(8,128)(2,1)} %all-gather.2.cloned.1.call-done.far, bf16[2,256,2048]{2,1,0:T(8,128)(2,1)} %v_pp.1, f32[2,256,512]{2,1,0:T(8,128)} %shard_map.101.ladder, ...), custom_call_target="tpu_custom_call" | custom-call | flops 536870912 | bytes 10485760 | tf_op jit(solution)/shard_map/pallas_call | solution.py:19
  (106 shorter events, 23.5 us)
Async XLA Ops:
  6.5 22.0 %copy-start.18 = (s32[8]{0:T(128)S(1)}, s32[8]{0:T(128)}, u32[]{:S(2)}) copy-start(s32[8]{0:T(128)} %constant.124.clone) | copy-start | bytes 100
  6.5 22.6 %copy-start.17 = (s32[2]{0:T(128)S(1)}, s32[2]{0:T(128)}, u32[]{:S(2)}) copy-start(s32[2]{0:T(128)} %param.16) | copy-start | bytes 28
  6.5 23.1 %copy-start.16 = (f32[2,256]{1,0:T(2,128)S(1)}, f32[2,256]{1,0:T(2,128)}, u32[]{:S(2)}) copy-start(f32[2,256]{1,0:T(2,128)} %param.17) | copy-start | bytes 6148
  6.5 24.0 %copy-start.15 = (f32[2,768]{1,0:T(2,128)S(1)}, f32[2,768]{1,0:T(2,128)}, u32[]{:S(2)}) copy-start(f32[2,768]{1,0:T(2,128)} %param.18) | copy-start | bytes 18436
  6.5 162.0 %all-gather.2.cloned.1.call-start = ((), (), s32[]{:S(2)}) async-start(), calls=%async_computation.6 | async-start | bytes 2359296 | tf_op jit(solution)/shard_map/all_gather | solution.py:232
  12.4 19.5 %collective-permute-start = (bf16[33,16,512]{2,1,0:T(8,128)(2,1)}, bf16[33,16,512]{2,1,0:T(8,128)(2,1)S(1)}, u32[]{:S(2)}, u32[]{:S(2)}) collective-permute-start(bf16[33,16,512]{2,1,0:T(8,128)(2,1)} %get-tuple-element.7.refs_0_), channel_id=1, source_target_pairs={{0,1},{1,2},{2,3},{3,4},{4,5},{5,6},{6,7},{7,0},{8,9},{9,10},{10,1... | collective-permute-start | bytes 1622024 | tf_op jit(solution)/shard_map/ppermute | solution.py:170
  14.9 17.0 %collective-permute-start.1 = (bf16[33,16,512]{2,1,0:T(8,128)(2,1)}, bf16[33,16,512]{2,1,0:T(8,128)(2,1)S(1)}, u32[]{:S(2)}, u32[]{:S(2)}) collective-permute-start(bf16[33,16,512]{2,1,0:T(8,128)(2,1)} %get-tuple-element.7.refs_0_), channel_id=1, source_target_pairs={{1,0},{2,1},{3,2},{4,3},{5,4},{6,5},{7,6},{0,7},{9,8},{10,9},{11,1... | collective-permute-start | bytes 1622024 | tf_op jit(solution)/shard_map/ppermute | solution.py:170
  20.5 23.5 %all-to-all-start = ((bf16[32,16,896]{2,1,0:T(8,128)(2,1)}), bf16[32,16,896]{2,1,0:T(8,128)(2,1)S(1)}, u32[]{:S(2)}, u32[]{:S(2)}) async-start(bf16[32,16,896]{2,1,0:T(8,128)(2,1)} %get-tuple-element.8), calls=%async_computation | async-start | bytes 1835008 | tf_op jit(solution)/shard_map/all_to_all | solution.py:171
  33.2 26.5 %collective-permute-start.2 = (bf16[33,16,512]{2,1,0:T(8,128)(2,1)S(1)}, bf16[33,16,512]{2,1,0:T(8,128)(2,1)}, u32[]{:S(2)}, u32[]{:S(2)}) collective-permute-start(bf16[33,16,512]{2,1,0:T(8,128)(2,1)S(1)} %collective-permute-done.refs_1_), channel_id=1, source_target_pairs={{0,1},{1,2},{2,3},{3,4},{4,5},{5,6},{6,7},{7,0},{8,9},{9,10},{10,1... | collective-permute-start | bytes 1622024 | tf_op jit(solution)/shard_map/ppermute | solution.py:181
  33.2 25.1 %collective-permute-start.3 = (bf16[33,16,512]{2,1,0:T(8,128)(2,1)S(1)}, bf16[33,16,512]{2,1,0:T(8,128)(2,1)}, u32[]{:S(2)}, u32[]{:S(2)}) collective-permute-start(bf16[33,16,512]{2,1,0:T(8,128)(2,1)S(1)} %collective-permute-done.1.refs_2_), channel_id=1, source_target_pairs={{1,0},{2,1},{3,2},{4,3},{5,4},{6,5},{7,6},{0,7},{9,8},{10,9},{11,1... | collective-permute-start | bytes 1622024 | tf_op jit(solution)/shard_map/ppermute | solution.py:181
  44.0 30.0 %all-to-all-start.1 = ((bf16[32,2,16,512]{3,2,1,0:T(8,128)(2,1)}), bf16[32,2,16,512]{3,2,1,0:T(8,128)(2,1)S(1)}, u32[]{:S(2)}, u32[]{:S(2)}) async-start(bf16[32,2,16,512]{3,2,1,0:T(8,128)(2,1)} %copy.30), calls=%async_computation.1 | async-start | bytes 2097152 | tf_op jit(solution)/shard_map/all_to_all | solution.py:189
  51.2 20.1 %collective-permute-start.7 = (bf16[33,16,256]{2,1,0:T(8,128)(2,1)}, bf16[33,16,256]{2,1,0:T(8,128)(2,1)S(1)}, u32[]{:S(2)}, u32[]{:S(2)}) collective-permute-start(bf16[33,16,256]{2,1,0:T(8,128)(2,1)} %shard_map.102.rest_0_), channel_id=1, source_target_pairs={{0,1},{1,2},{2,3},{3,4},{4,5},{5,6},{6,7},{7,0},{8,9},{9,10},{10,1... | collective-permute-start | bytes 811016 | tf_op jit(solution)/shard_map/ppermute | solution.py:180
  51.2 20.1 %collective-permute-start.8 = (bf16[33,16,256]{2,1,0:T(8,128)(2,1)}, bf16[33,16,256]{2,1,0:T(8,128)(2,1)}, u32[]{:S(2)}, u32[]{:S(2)}) collective-permute-start(bf16[33,16,256]{2,1,0:T(8,128)(2,1)} %shard_map.102.rest_0_), channel_id=1, source_target_pairs={{1,0},{2,1},{3,2},{4,3},{5,4},{6,5},{7,6},{0,7},{9,8},{10,9},{11,1... | collective-permute-start | bytes 811016 | tf_op jit(solution)/shard_map/ppermute | solution.py:180
  62.0 32.1 %collective-permute-start.4 = (bf16[33,16,512]{2,1,0:T(8,128)(2,1)}, bf16[33,16,512]{2,1,0:T(8,128)(2,1)S(1)}, u32[]{:S(2)}, u32[]{:S(2)}) collective-permute-start(bf16[33,16,512]{2,1,0:T(8,128)(2,1)} %collective-permute-done.2.refs_3_), channel_id=1, source_target_pairs={{0,1},{1,2},{2,3},{3,4},{4,5},{5,6},{6,7},{7,0},{8,9},{9,10},{10,1... | collective-permute-start | bytes 1622024 | tf_op jit(solution)/shard_map/ppermute | solution.py:183
  62.5 31.6 %collective-permute-start.5 = (bf16[33,16,512]{2,1,0:T(8,128)(2,1)}, bf16[33,16,512]{2,1,0:T(8,128)(2,1)S(1)}, u32[]{:S(2)}, u32[]{:S(2)}) collective-permute-start(bf16[33,16,512]{2,1,0:T(8,128)(2,1)} %collective-permute-done.3.refs_4_), channel_id=1, source_target_pairs={{1,0},{2,1},{3,2},{4,3},{5,4},{6,5},{7,6},{0,7},{9,8},{10,9},{11,1... | collective-permute-start | bytes 1622024 | tf_op jit(solution)/shard_map/ppermute | solution.py:183
  71.3 22.8 %copy-start.11 = (bf16[33,16,256]{2,1,0:T(8,128)(2,1)}, bf16[33,16,256]{2,1,0:T(8,128)(2,1)S(1)}, u32[]{:S(2)}) copy-start(bf16[33,16,256]{2,1,0:T(8,128)(2,1)S(1)} %collective-permute-done.7.rest_1_) | copy-start | bytes 811012
  71.3 19.3 %collective-permute-start.9 = (bf16[33,16,256]{2,1,0:T(8,128)(2,1)S(1)}, bf16[33,16,256]{2,1,0:T(8,128)(2,1)}, u32[]{:S(2)}, u32[]{:S(2)}) collective-permute-start(bf16[33,16,256]{2,1,0:T(8,128)(2,1)S(1)} %collective-permute-done.7.rest_1_), channel_id=1, source_target_pairs={{0,1},{1,2},{2,3},{3,4},{4,5},{5,6},{6,7},{7,0},{8,9},{9,10},{10,1... | collective-permute-start | bytes 811016 | tf_op jit(solution)/shard_map/ppermute | solution.py:182
  71.4 19.3 %collective-permute-start.10 = (bf16[33,16,256]{2,1,0:T(8,128)(2,1)}, bf16[33,16,256]{2,1,0:T(8,128)(2,1)}, u32[]{:S(2)}, u32[]{:S(2)}) collective-permute-start(bf16[33,16,256]{2,1,0:T(8,128)(2,1)} %collective-permute-done.8.rest_2_), channel_id=1, source_target_pairs={{1,0},{2,1},{3,2},{4,3},{5,4},{6,5},{7,6},{0,7},{9,8},{10,9},{11,1... | collective-permute-start | bytes 811016 | tf_op jit(solution)/shard_map/ppermute | solution.py:182
  74.0 20.1 %copy-start.1 = (bf16[32,2,16,512]{3,2,1,0:T(8,128)(2,1)}, bf16[32,2,16,512]{3,2,1,0:T(8,128)(2,1)S(1)}, u32[]{:S(2)}) copy-start(bf16[32,2,16,512]{3,2,1,0:T(8,128)(2,1)S(1)} %all-to-all-done.1.pair_a) | copy-start | bytes 3145732
  74.0 26.1 %all-to-all-start.2 = ((bf16[32,2,16,512]{3,2,1,0:T(8,128)(2,1)}), bf16[32,2,16,512]{3,2,1,0:T(8,128)(2,1)S(1)}, u32[]{:S(2)}, u32[]{:S(2)}) async-start(bf16[32,2,16,512]{3,2,1,0:T(8,128)(2,1)} %copy.31), calls=%async_computation.2 | async-start | bytes 2097152 | tf_op jit(solution)/shard_map/all_to_all | solution.py:189
  90.7 18.0 %collective-permute-start.11 = (bf16[33,16,256]{2,1,0:T(8,128)(2,1)}, bf16[33,16,256]{2,1,0:T(8,128)(2,1)}, u32[]{:S(2)}, u32[]{:S(2)}) collective-permute-start(bf16[33,16,256]{2,1,0:T(8,128)(2,1)} %collective-permute-done.9.rest_3_), channel_id=1, source_target_pairs={{0,1},{1,2},{2,3},{3,4},{4,5},{5,6},{6,7},{7,0},{8,9},{9,10},{10,1... | collective-permute-start | bytes 811016 | tf_op jit(solution)/shard_map/ppermute | solution.py:184
  90.7 15.3 %collective-permute-start.12 = (bf16[33,16,256]{2,1,0:T(8,128)(2,1)}, bf16[33,16,256]{2,1,0:T(8,128)(2,1)}, u32[]{:S(2)}, u32[]{:S(2)}) collective-permute-start(bf16[33,16,256]{2,1,0:T(8,128)(2,1)} %collective-permute-done.10.rest_4_), channel_id=1, source_target_pairs={{1,0},{2,1},{3,2},{4,3},{5,4},{6,5},{7,6},{0,7},{9,8},{10,9},{11,1... | collective-permute-start | bytes 811016 | tf_op jit(solution)/shard_map/ppermute | solution.py:184
  94.1 11.3 %copy-start.8 = (bf16[33,16,512]{2,1,0:T(8,128)(2,1)}, bf16[33,16,512]{2,1,0:T(8,128)(2,1)S(1)}, u32[]{:S(2)}) copy-start(bf16[33,16,512]{2,1,0:T(8,128)(2,1)S(1)} %collective-permute-done.5.refs_6_) | copy-start | bytes 1622020
  100.1 21.2 %copy-start.2 = (bf16[32,2,16,512]{3,2,1,0:T(8,128)(2,1)}, bf16[32,2,16,512]{3,2,1,0:T(8,128)(2,1)S(1)}, u32[]{:S(2)}) copy-start(bf16[32,2,16,512]{3,2,1,0:T(8,128)(2,1)S(1)} %all-to-all-done.2.pair_b) | copy-start | bytes 3145732
  100.1 21.1 %all-to-all-start.3 = ((bf16[32,2,16,512]{3,2,1,0:T(8,128)(2,1)}), bf16[32,2,16,512]{3,2,1,0:T(8,128)(2,1)S(1)}, u32[]{:S(2)}, u32[]{:S(2)}) async-start(bf16[32,2,16,512]{3,2,1,0:T(8,128)(2,1)} %copy.32), calls=%async_computation.3 | async-start | bytes 2097152 | tf_op jit(solution)/shard_map/all_to_all | solution.py:189
  104.8 14.9 %collective-permute-start.6 = (bf16[33,16,512]{2,1,0:T(8,128)(2,1)S(1)}, bf16[33,16,512]{2,1,0:T(8,128)(2,1)S(1)}, u32[]{:S(2)}, u32[]{:S(2)}) collective-permute-start(bf16[33,16,512]{2,1,0:T(8,128)(2,1)S(1)} %collective-permute-done.4.refs_5_), channel_id=1, source_target_pairs={{0,1},{1,2},{2,3},{3,4},{4,5},{5,6},{6,7},{7,0},{8,9},{9,10},{10,1... | collective-permute-start | bytes 1622024 | tf_op jit(solution)/shard_map/ppermute | solution.py:185
  106.0 23.4 %collective-permute-start.13 = (bf16[33,16,256]{2,1,0:T(8,128)(2,1)}, bf16[33,16,256]{2,1,0:T(8,128)(2,1)S(1)}, u32[]{:S(2)}, u32[]{:S(2)}) collective-permute-start(bf16[33,16,256]{2,1,0:T(8,128)(2,1)} %collective-permute-done.12.rest_6_), channel_id=1, source_target_pairs={{1,0},{2,1},{3,2},{4,3},{5,4},{6,5},{7,6},{0,7},{9,8},{10,9},{11,1... | collective-permute-start | bytes 811016 | tf_op jit(solution)/shard_map/ppermute | solution.py:186
  121.3 19.7 %copy-start.3 = (bf16[32,2,16,512]{3,2,1,0:T(8,128)(2,1)}, bf16[32,2,16,512]{3,2,1,0:T(8,128)(2,1)S(1)}, u32[]{:S(2)}) copy-start(bf16[32,2,16,512]{3,2,1,0:T(8,128)(2,1)S(1)} %all-to-all-done.3.pair_c) | copy-start | bytes 3145732
  121.3 19.7 %all-to-all-start.4 = ((bf16[32,16,512]{2,1,0:T(8,128)(2,1)}), bf16[32,16,512]{2,1,0:T(8,128)(2,1)S(1)}, u32[]{:S(2)}, u32[]{:S(2)}) async-start(bf16[32,16,512]{2,1,0:T(8,128)(2,1)} %slice.145), calls=%async_computation.4 | async-start | bytes 1048576 | tf_op jit(solution)/shard_map/all_to_all | solution.py:192
  129.4 11.6 %copy-start.12 = (bf16[33,16,256]{2,1,0:T(8,128)(2,1)}, bf16[33,16,256]{2,1,0:T(8,128)(2,1)S(1)}, u32[]{:S(2)}) copy-start(bf16[33,16,256]{2,1,0:T(8,128)(2,1)S(1)} %collective-permute-done.13.rest_7_) | copy-start | bytes 811012
  131.0 23.3 %copy-start.14 = (bf16[8,16,256]{2,1,0:T(8,128)(2,1)S(1)}, bf16[8,16,256]{2,1,0:T(8,128)(2,1)}, u32[]{:S(2)}) copy-start(bf16[8,16,256]{2,1,0:T(8,128)(2,1)} %constant_dynamic-update-slice_fusion.1) | copy-start | bytes 196612
  150.6 17.9 %all-to-all-start.5 = ((bf16[32,16,768]{2,1,0:T(8,128)(2,1)}), bf16[32,16,768]{2,1,0:T(8,128)(2,1)S(1)}, u32[]{:S(2)}, u32[]{:S(2)}) async-start(bf16[32,16,768]{2,1,0:T(8,128)(2,1)} %shard_map.103), calls=%async_computation.5 | async-start | bytes 1572864 | tf_op jit(solution)/shard_map/all_to_all | solution.py:221
  (8 other events, 34.4 us)
Sparse Core Ops, SparseCore 0:
  20.6 54.6 all-gather.1

commit v2 on v0

v2 whole, which is shorter than its diff:
```python
import functools

import jax
import jax.numpy as jnp
from jax import lax
from jax.experimental import pallas as pl
from jax.experimental.pallas import tpu as pltpu
from jax.sharding import PartitionSpec as P

META = 128
VMEM_LIMIT = 56 * 1024 * 1024

F32, BF16, I32 = jnp.float32, jnp.bfloat16, jnp.int32


def call(kernel, outs, operands, scalars=(), scratch=(), flops=0, moved=0):
    smem, vmem = pl.BlockSpec(memory_space=pltpu.SMEM), pl.BlockSpec(memory_space=pltpu.VMEM)
    return pl.pallas_call(
        kernel,
        out_shape=outs,
        in_specs=[smem] * len(scalars) + [vmem] * len(operands),
        out_specs=jax.tree.map(lambda _: vmem, outs),
        scratch_shapes=list(scratch),
        compiler_params=pltpu.CompilerParams(vmem_limit_bytes=VMEM_LIMIT),
        cost_estimate=pl.CostEstimate(flops=flops, bytes_accessed=moved, transcendentals=0),
    )(*scalars, *operands)


def tables(count):
    return (
        pltpu.VMEM((count, 8, META), I32),
        pltpu.SMEM((count, 8, META), I32),
        pltpu.SemaphoreType.DMA,
    )


def to_scalars(vector, scalar, sem):
    copy = pltpu.make_async_copy(vector, scalar, sem)
    copy.start()
    copy.wait()


def pack_kernel(blocks, target, coef, amp, items):
    count, rows, width = amp.shape
    ch_dev, nb_tile = target.shape
    factor = coef[...].astype(F32)
    for b in range(count):
        ch, j = divmod(b, nb_tile)
        to = lax.div(target[ch, j], ch_dev * blocks)
        slot = lax.rem(target[ch, j], ch_dev * blocks)
        scaled = amp[b].astype(F32) * factor[ch : ch + 1, j : j + 1]
        items[to, :, :width] = scaled.astype(BF16)
        items[to, :, width:] = jnp.full((rows, META), slot.astype(F32)).astype(BF16)


def settle_kernel(blocks, got, placed, homes, slot_v, slot, sem):
    count, rows, wide = got.shape
    width = wide - META
    nb_tile = count // 2
    lane = lax.broadcasted_iota(I32, (rows, META), 1)
    notes = jnp.zeros((rows, META), F32)
    for c in range(count):
        notes = jnp.where(lane == c, got[c, :, width:].astype(F32), notes)
    at = notes[:8].astype(I32)
    homes[...] = lax.div(at, blocks) * nb_tile + lax.rem(at, nb_tile)
    slot_v[0] = homes[...]
    to_scalars(slot_v, slot, sem)
    for c in range(count):
        placed[slot[0, 0, c]] = got[c, :, :width]


def tile_at(step):
    n = lax.axis_size("tile")
    return lax.rem(lax.axis_index("tile") + step + n, n)


STEPS = (0, -1, 1, -2, 2, -3, 3, 4)


def gather_rows(pieces, placed):
    ch_dev, total, width = placed.shape
    per = total // len(STEPS)
    each = pieces[0].shape[0] // ch_dev
    for piece, ref in enumerate(pieces):
        at = pl.ds(pl.multiple_of(tile_at(STEPS[piece]) * per, per), per)
        for ch in range(ch_dev):
            placed[ch, at] = ref[ch * each : (ch + 1) * each].reshape(per, width)
    at = pl.ds(pl.multiple_of(tile_at(STEPS[-1]) * per, per), per)
    for ch in range(ch_dev):
        placed[ch, at] = jnp.zeros((per, width), BF16)


def most_kernel(*refs):
    pieces, (matrix, part, placed) = refs[: len(STEPS) - 1], refs[len(STEPS) - 1 :]
    gather_rows(pieces, placed)
    for ch in range(placed.shape[0]):
        part[ch] = jnp.dot(matrix[ch], placed[ch], preferred_element_type=F32)


def rest_of(ch, halves, matrix):
    per, width = matrix.shape[1], halves[0].shape[2]
    columns = pl.ds(pl.multiple_of(tile_at(STEPS[-1]) * per, per), per)
    last = halves[ch][...].reshape(per, width)
    return jnp.dot(matrix[ch, :, columns], last, preferred_element_type=F32)


def back_kernel(homes, half_a, half_b, part, w_ph, back, result, slot_v, slot, sem):
    count, rows, _ = back.shape
    ch_dev, per, width = part.shape
    slot_v[0] = homes[...]
    to_scalars(slot_v, slot, sem)
    for ch in range(ch_dev):
        total = part[ch] + rest_of(ch, (half_a, half_b), w_ph)
        result[ch * per : (ch + 1) * per] = total.astype(BF16)
    for c in range(count):
        row = pl.ds(pl.multiple_of(slot[0, 0, c] * rows, rows), rows)
        back[c] = result[row, :]


def ladder_kernel(half_a, half_b, part, v_pp, v_pphh, ladder):
    for ch in range(part.shape[0]):
        total = part[ch] + rest_of(ch, (half_a, half_b), v_pp)
        ladder[ch] = v_pphh[ch].astype(F32) + total


def final_kernel(blocks, target, live, coef, ladder, back, e_part, e_hole, out):
    ch_dev, per, width = out.shape
    count, rows, _ = back.shape
    nb_tile = count // ch_dev
    first = lax.axis_index("tile") * per
    factor = coef[...].astype(F32)
    for ch in range(ch_dev):
        for b in range(nb_tile):
            at = slice(b * rows, (b + 1) * rows)
            own = lax.div(target[ch, b], ch_dev * blocks)
            come = back[own].astype(F32) * factor[ch : ch + 1, b : b + 1]
            sums = ladder[ch, at] + come
            denom = e_part[ch, at] + e_hole[ch]
            row = lax.broadcasted_iota(I32, (rows, width), 0) + (first + b * rows)
            out[ch, at] = jnp.where(row < live[ch], sums / denom, 0.0).astype(BF16)


def after(x, *others):
    return lax.optimization_barrier((x, *others))[0]


def body(amp, v_pphh, v_pp, w_ph, coef, target, pp_size, e_part, e_hole):
    ch_dev, tile_rows, width = amp.shape
    nb_tile = target.shape[1]
    rows = tile_rows // nb_tile
    n_tile = lax.axis_size("tile")
    blocks = nb_tile * n_tile
    count = ch_dev * nb_tile
    total = tile_rows * n_tile
    right = [(i, (i + 1) % n_tile) for i in range(n_tile)]
    left = [((i + 1) % n_tile, i) for i in range(n_tile)]
    to_right = functools.partial(lax.ppermute, axis_name="tile", perm=right)
    to_left = functools.partial(lax.ppermute, axis_name="tile", perm=left)

    def both(a, b):
        return to_right(a), to_left(b)

    exchange = functools.partial(
        lax.all_to_all, axis_name="chan", split_axis=0, concat_axis=0, tiled=True
    )

    own_rows = amp.reshape(count, rows, width)
    block_type = jax.ShapeDtypeStruct((count, rows, width), BF16)
    part_type = jax.ShapeDtypeStruct((ch_dev, tile_rows, width), F32)
    amp1 = both(own_rows, own_rows)
    items = call(
        functools.partial(pack_kernel, blocks),
        jax.ShapeDtypeStruct((count, rows, width + META), BF16),
        (coef, own_rows),
        (target,),
        moved=4 * 2**20,
    )
    far, homes = call(
        functools.partial(settle_kernel, blocks),
        (block_type, jax.ShapeDtypeStruct((8, META), I32)),
        (after(exchange(items), amp1),),
        scratch=tables(1),
        moved=4 * 2**20,
    )
    far1 = both(far, far)
    amp2 = both(*after(amp1))
    far2 = both(*after(far1))
    far3 = both(*after(far2))
    far4 = both(far3[0][: count // 2], far3[1][count // 2 :])
    def most(pieces, matrix):
        return call(
            most_kernel,
            part_type,
            (*pieces, matrix),
            scratch=(pltpu.VMEM((ch_dev, total, width), BF16),),
            flops=2 * ch_dev * tile_rows * total * width,
            moved=12 * 2**20,
        )

    cycle_most = most((far, *far1, *far2, *far3), w_ph)
    amp3 = both(*after(amp2, cycle_most, far4))
    back = call(
        back_kernel,
        block_type,
        (homes, *far4, cycle_most, w_ph),
        scratch=(pltpu.VMEM((ch_dev * tile_rows, width), BF16), *tables(1)),
        flops=2 * ch_dev * tile_rows * tile_rows * width,
        moved=6 * 2**20,
    )
    returned = exchange(back)
    amp3 = after(amp3, back)
    amp4 = both(amp3[0][: count // 2], amp3[1][count // 2 :])
    ladder = call(
        ladder_kernel,
        part_type,
        (*amp4, most((own_rows, *amp1, *amp2, *amp3), v_pp), v_pp, v_pphh),
        flops=2 * ch_dev * tile_rows * tile_rows * width,
        moved=6 * 2**20,
    )
    return call(
        functools.partial(final_kernel, blocks),
        jax.ShapeDtypeStruct((ch_dev, tile_rows, width), BF16),
        (coef, ladder, returned, e_part[:, :, None], e_hole[:, None, :]),
        (target, pp_size),
        flops=10 * ch_dev * tile_rows * width,
        moved=6 * 2**20,
    )


def solution(mesh):
    placed = (
        P("chan", "tile", None),
        P("chan", "tile", None),
        P("chan", "tile", None),
        P("chan", "tile", None),
        P("chan", "tile"),
        P("chan", "tile"),
        P("chan"),
        P("chan", "tile"),
        P("chan", None),
    )
    return jax.shard_map(
        body, mesh=mesh, in_specs=placed, out_specs=P("chan", "tile", None), check_vma=False
    )
```

time: 243 us -> 160 us (0.66)
  waiting for transfers between devices: 119 us -> 78.8 us
  Pallas kernels: 0 us -> 29.8 us
  blocking collectives: 28.3 us -> 0 us
  other arithmetic: 17 us -> 0 us
  local copies, waits for them, and re-layouts: 20.1 us -> 4.21 us
  between operations: 13.6 us -> 0.23 us
  matrix products: 11.2 us -> 0 us
  starting transfers between devices: 33.5 us -> 44.4 us
    all_to_all x3 -> x2, waiting for transfers between devices: 83.3 us -> 0.01 us  [the longest x1 0.01 us: body(): exchange(items)]
    ppermute x0 -> x16, waiting for transfers between devices: none -> 78.8 us  [both(): return (to_right(a), to_left(b))]
    all_gather x1 -> x0, waiting for transfers between devices: 34.7 us -> none  [body(): lax.all_gather(amp, 'tile', axis=1, tiled=True)]
    pallas_call x0 -> x7, Pallas kernels: none -> 29.8 us  [call(): pl.pallas_call(kernel, out_shape=outs, in_specs=[smem] * len(scalars) + [...]
    all_gather x2 -> x0, blocking collectives: 28.3 us -> none  [the longest x1 16.7 us: body(): lax.all_gather(target, 'tile', axis=1, tiled=True)]
    ppermute x0 -> x16, starting transfers between devices: none -> 25.2 us  [both(): return (to_right(a), to_left(b))]
    gather x5 -> x0, local copies, waits for them, and re-layouts: 17.6 us -> none  [the longest x1 6.35 us: body(): arrived[jnp.argsort(arrived_slots)].reshape(ch_dev, blocks * rows, width)]
    all_to_all x3 -> x2, starting transfers between devices: 33.5 us -> 19.2 us  [the longest x1 10.6 us: body(): returned = exchange(back)]
  transfers between devices with their start and end apart: 4 -> 18, of which waited for: 3 -> 6; matrix products, arithmetic and copies ran while one was open for 11% -> 1% of each run, Pallas kernels for 0% -> 14%
where the time goes in v2:
time: 160 us; the launch traced here: 157 us
  waiting for transfers between devices  78.8 us (49%)
  starting transfers between devices  44.4 us (28%)
  Pallas kernels  29.8 us (19%)
  local copies, waits for them, and re-layouts  4.21 us (3%)
    ppermute x16, waiting for transfers between devices, both(): return (to_right(a), to_left(b))  78.8 us
    pallas_call x7, Pallas kernels, call(): pl.pallas_call(kernel, out_shape=outs, in_specs=[smem] * len(scalars) + [...  29.8 us
    ppermute x16, starting transfers between devices, both(): return (to_right(a), to_left(b))  25.2 us
    all_to_all x1, starting transfers between devices, body(): returned = exchange(back)  10.6 us
    all_to_all x1, starting transfers between devices, body(): exchange(items)  8.59 us
  transfers between devices with their start and end apart: 18, of which 6 were waited for; matrix products, arithmetic and copies ran while one was open for 1% of the time, Pallas kernels for 14%

profile of v2, /device:TPU:1, one launch (start us, length us, event | category | flops | bytes accessed | tf_op | source)
XLA Modules:
  0.0 157.4 jit_solution(2236072680165767884)
XLA Ops:
  0.0 2.4 %shard_map.91 = bf16[32,16,896]{2,1,0:T(8,128)(2,1)} custom-call(s32[2,16]{1,0:T(2,128)} %target.3, bf16[2,16]{1,0:T(2,128)(2,1)} %coef.3, bf16[32,16,768]{2,1,0:T(8,128)(2,1)} %bitcast.2), custom_call_target="tpu_custom_call" | custom-call | bytes 4194304 | tf_op jit(solution)/shard_map/pallas_call | solution.py:18
  2.4 8.6 %all-to-all-start = ((bf16[32,16,896]{2,1,0:T(8,128)(2,1)}), bf16[32,16,896]{2,1,0:T(8,128)(2,1)S(1)}, u32[]{:S(2)}, u32[]{:S(2)}) async-start(bf16[32,16,896]{2,1,0:T(8,128)(2,1)} %shard_map.91), calls=%async_computation | async-start | bytes 1835008 | tf_op jit(solution)/shard_map/all_to_all | solution.py:181
  11.0 1.7 %collective-permute-start = (bf16[32,16,768]{2,1,0:T(8,128)(2,1)S(1)}, bf16[32,16,768]{2,1,0:T(8,128)(2,1)S(1)}, u32[]{:S(2)}, u32[]{:S(2)}) collective-permute-start(bf16[32,16,768]{2,1,0:T(8,128)(2,1)S(1)} %bitcast.4), channel_id=1, source_target_pairs={{0,1},{1,2},{2,3},{3,4},{4,5},{5,6},{6,7},{7,0},{8,9},{9,10},{10,1... | collective-permute-start | bytes 2359304 | tf_op jit(solution)/shard_map/ppermute | solution.py:161
  12.7 4.0 %collective-permute-start.1 = (bf16[32,16,768]{2,1,0:T(8,128)(2,1)S(1)}, bf16[32,16,768]{2,1,0:T(8,128)(2,1)}, u32[]{:S(2)}, u32[]{:S(2)}) collective-permute-start(bf16[32,16,768]{2,1,0:T(8,128)(2,1)S(1)} %bitcast.5), channel_id=1, source_target_pairs={{1,0},{2,1},{3,2},{4,3},{5,4},{6,5},{7,6},{0,7},{9,8},{10,9},{11,1... | collective-permute-start | bytes 2359304 | tf_op jit(solution)/shard_map/ppermute | solution.py:161
  16.8 17.7 %collective-permute-done.refs_1_ = bf16[32,16,768]{2,1,0:T(8,128)(2,1)S(1)} collective-permute-done((bf16[32,16,768]{2,1,0:T(8,128)(2,1)S(1)}, bf16[32,16,768]{2,1,0:T(8,128)(2,1)S(1)}, u32[]{:S(2)}, u32[]{:S(2)}) %collective-permute-start) | collective-permute-done | bytes 786464 | tf_op jit(solution)/shard_map/ppermute | solution.py:161
  34.5 1.0 copy-done
  35.4 2.8 %shard_map.92 = (bf16[32,16,768]{2,1,0:T(8,128)(2,1)}, s32[8,128]{1,0:T(8,128)}) custom-call(bf16[32,16,896]{2,1,0:T(8,128)(2,1)} %copy-done), custom_call_target="tpu_custom_call" | custom-call | bytes 4194304 | tf_op jit(solution)/shard_map/pallas_call | solution.py:18
  38.3 2.7 %collective-permute-start.5 = (bf16[32,16,768]{2,1,0:T(8,128)(2,1)}, bf16[32,16,768]{2,1,0:T(8,128)(2,1)S(1)}, u32[]{:S(2)}, u32[]{:S(2)}) collective-permute-start(bf16[32,16,768]{2,1,0:T(8,128)(2,1)} %get-tuple-element.21.refs_0_), channel_id=1, source_target_pairs={{1,0},{2,1},{3,2},{4,3},{5,4},{6,5},{7,6},{0,7},{9,8},{10,9},{11,1... | collective-permute-start | bytes 2359304 | tf_op jit(solution)/shard_map/ppermute | solution.py:161
  41.0 17.1 %collective-permute-done.4.refs_1_ = bf16[32,16,768]{2,1,0:T(8,128)(2,1)S(1)} collective-permute-done((bf16[32,16,768]{2,1,0:T(8,128)(2,1)}, bf16[32,16,768]{2,1,0:T(8,128)(2,1)S(1)}, u32[]{:S(2)}, u32[]{:S(2)}) %collective-permute-start.4) | collective-permute-done | bytes 786464 | tf_op jit(solution)/shard_map/ppermute | solution.py:161
  58.1 0.9 collective-permute-start.6
  59.0 1.8 %collective-permute-start.7 = (bf16[32,16,768]{2,1,0:T(8,128)(2,1)S(1)}, bf16[32,16,768]{2,1,0:T(8,128)(2,1)S(1)}, u32[]{:S(2)}, u32[]{:S(2)}) collective-permute-start(bf16[32,16,768]{2,1,0:T(8,128)(2,1)S(1)} %collective-permute-done.5.refs_2_), channel_id=1, source_target_pairs={{1,0},{2,1},{3,2},{4,3},{5,4},{6,5},{7,6},{0,7},{9,8},{10,9},{11,1... | collective-permute-start | bytes 2359304 | tf_op jit(solution)/shard_map/ppermute | solution.py:161
  60.8 16.0 %collective-permute-done.6.refs_3_ = bf16[32,16,768]{2,1,0:T(8,128)(2,1)S(1)} collective-permute-done((bf16[32,16,768]{2,1,0:T(8,128)(2,1)S(1)}, bf16[32,16,768]{2,1,0:T(8,128)(2,1)S(1)}, u32[]{:S(2)}, u32[]{:S(2)}) %collective-permute-start.6) | collective-permute-done | bytes 786464 | tf_op jit(solution)/shard_map/ppermute | solution.py:161
  76.8 0.2 collective-permute-start.8
  77.0 2.5 %collective-permute-start.9 = (bf16[32,16,768]{2,1,0:T(8,128)(2,1)S(1)}, bf16[32,16,768]{2,1,0:T(8,128)(2,1)S(1)}, u32[]{:S(2)}, u32[]{:S(2)}) collective-permute-start(bf16[32,16,768]{2,1,0:T(8,128)(2,1)S(1)} %collective-permute-done.7.refs_4_), channel_id=1, source_target_pairs={{1,0},{2,1},{3,2},{4,3},{5,4},{6,5},{7,6},{0,7},{9,8},{10,9},{11,1... | collective-permute-start | bytes 2359304 | tf_op jit(solution)/shard_map/ppermute | solution.py:161
  79.5 2.7 %collective-permute-start.3 = (bf16[32,16,768]{2,1,0:T(8,128)(2,1)}, bf16[32,16,768]{2,1,0:T(8,128)(2,1)}, u32[]{:S(2)}, u32[]{:S(2)}) collective-permute-start(bf16[32,16,768]{2,1,0:T(8,128)(2,1)} %collective-permute-done.1.refs_2_), channel_id=1, source_target_pairs={{1,0},{2,1},{3,2},{4,3},{5,4},{6,5},{7,6},{0,7},{9,8},{10,9},{11,1... | collective-permute-start | bytes 2359304 | tf_op jit(solution)/shard_map/ppermute | solution.py:161
  82.2 12.4 %collective-permute-done.8.refs_5_ = bf16[32,16,768]{2,1,0:T(8,128)(2,1)S(1)} collective-permute-done((bf16[32,16,768]{2,1,0:T(8,128)(2,1)S(1)}, bf16[32,16,768]{2,1,0:T(8,128)(2,1)S(1)}, u32[]{:S(2)}, u32[]{:S(2)}) %collective-permute-start.8) | collective-permute-done | bytes 786464 | tf_op jit(solution)/shard_map/ppermute | solution.py:161
  94.7 2.7 %collective-permute-start.11 = (bf16[16,16,768]{2,1,0:T(8,128)(2,1)S(1)}, bf16[16,16,768]{2,1,0:T(8,128)(2,1)S(1)}, u32[]{:S(2)}, u32[]{:S(2)}) collective-permute-start(bf16[16,16,768]{2,1,0:T(8,128)(2,1)S(1)} %slice.17), channel_id=1, source_target_pairs={{1,0},{2,1},{3,2},{4,3},{5,4},{6,5},{7,6},{0,7},{9,8},{10,9},{11,1... | collective-permute-start | bytes 1179656 | tf_op jit(solution)/shard_map/ppermute | solution.py:161
  97.5 6.7 %shard_map.93.part = f32[2,256,768]{2,1,0:T(8,128)} custom-call(bf16[32,16,768]{2,1,0:T(8,128)(2,1)} %get-tuple-element.21.refs_0_, bf16[32,16,768]{2,1,0:T(8,128)(2,1)} %copy-done.8, bf16[32,16,768]{2,1,0:T(8,128)(2,1)} %copy-done.9, bf16[32,16,768]{2,1,0:T(8,128)(2,1)} %copy-done.10, bf16[32,16,768]{2,1,0:T(8,128)(2,1)} %copy-done.11, ...), custom_call_target="tpu_custom_call" | custom-call | flops 1610612736 | bytes 12582912 | tf_op jit(solution)/shard_map/pallas_call | solution.py:18
  104.2 7.4 %collective-permute-done.2.refs_3_ = bf16[32,16,768]{2,1,0:T(8,128)(2,1)} collective-permute-done((bf16[32,16,768]{2,1,0:T(8,128)(2,1)S(1)}, bf16[32,16,768]{2,1,0:T(8,128)(2,1)}, u32[]{:S(2)}, u32[]{:S(2)}) %collective-permute-start.2) | collective-permute-done | bytes 786464 | tf_op jit(solution)/shard_map/ppermute | solution.py:161
  111.5 8.3 %collective-permute-done.10.half_a = bf16[16,16,768]{2,1,0:T(8,128)(2,1)S(1)} collective-permute-done((bf16[16,16,768]{2,1,0:T(8,128)(2,1)S(1)}, bf16[16,16,768]{2,1,0:T(8,128)(2,1)S(1)}, u32[]{:S(2)}, u32[]{:S(2)}) %collective-permute-start.10) | collective-permute-done | bytes 393248 | tf_op jit(solution)/shard_map/ppermute | solution.py:161
  119.9 0.3 collective-permute-start.12
  120.1 2.7 %collective-permute-start.13 = (bf16[32,16,768]{2,1,0:T(8,128)(2,1)}, bf16[32,16,768]{2,1,0:T(8,128)(2,1)S(1)}, u32[]{:S(2)}, u32[]{:S(2)}) collective-permute-start(bf16[32,16,768]{2,1,0:T(8,128)(2,1)} %collective-permute-done.3.refs_4_), channel_id=1, source_target_pairs={{1,0},{2,1},{3,2},{4,3},{5,4},{6,5},{7,6},{0,7},{9,8},{10,9},{11,1... | collective-permute-start | bytes 2359304 | tf_op jit(solution)/shard_map/ppermute | solution.py:161
  122.8 4.3 %shard_map.94 = bf16[32,16,768]{2,1,0:T(8,128)(2,1)} custom-call(s32[8,128]{1,0:T(8,128)} %get-tuple-element.28.homes, bf16[16,16,768]{2,1,0:T(8,128)(2,1)} %copy-done.12, bf16[16,16,768]{2,1,0:T(8,128)(2,1)} %copy-done.13, f32[2,256,768]{2,1,0:T(8,128)} %shard_map.93.part, bf16[2,256,2048]{2,1,0:T(8,128)(2,1)} %w_ph.1), custom_call_target="tpu_custom_call" | custom-call | flops 201326592 | bytes 6291456 | tf_op jit(solution)/shard_map/pallas_call | solution.py:18
  127.1 10.6 %all-to-all-start.1 = ((bf16[32,16,768]{2,1,0:T(8,128)(2,1)}), bf16[32,16,768]{2,1,0:T(8,128)(2,1)S(1)}, u32[]{:S(2)}, u32[]{:S(2)}) async-start(bf16[32,16,768]{2,1,0:T(8,128)(2,1)} %shard_map.94), calls=%async_computation.1 | async-start | bytes 1572864 | tf_op jit(solution)/shard_map/all_to_all | solution.py:210
  137.9 2.7 %collective-permute-start.15 = (bf16[16,16,768]{2,1,0:T(8,128)(2,1)S(1)}, bf16[16,16,768]{2,1,0:T(8,128)(2,1)}, u32[]{:S(2)}, u32[]{:S(2)}) collective-permute-start(bf16[16,16,768]{2,1,0:T(8,128)(2,1)S(1)} %slice.15), channel_id=1, source_target_pairs={{1,0},{2,1},{3,2},{4,3},{5,4},{6,5},{7,6},{0,7},{9,8},{10,9},{11,1... | collective-permute-start | bytes 1179656 | tf_op jit(solution)/shard_map/ppermute | solution.py:161
  140.6 0.9 copy.10.e_part
  141.5 0.6 broadcast_in_dim.7.e_hole
  142.1 6.7 %shard_map.95.part = f32[2,256,768]{2,1,0:T(8,128)} custom-call(bf16[32,16,768]{2,1,0:T(8,128)(2,1)} %bitcast.3, bf16[32,16,768]{2,1,0:T(8,128)(2,1)} %copy-done.7, bf16[32,16,768]{2,1,0:T(8,128)(2,1)} %collective-permute-done.1.refs_2_, bf16[32,16,768]{2,1,0:T(8,128)(2,1)} %collective-permute-done.2.refs_3_, ...), custom_call_target="tpu_custom_call" | custom-call | flops 1610612736 | bytes 12582912 | tf_op jit(solution)/shard_map/pallas_call | solution.py:18
  148.7 0.7 copy-done.14
  149.5 4.0 %shard_map.96.ladder = f32[2,256,768]{2,1,0:T(8,128)} custom-call(bf16[16,16,768]{2,1,0:T(8,128)(2,1)} %copy-done.14, bf16[16,16,768]{2,1,0:T(8,128)(2,1)} %collective-permute-done.15.half_b, f32[2,256,768]{2,1,0:T(8,128)} %shard_map.95.part, bf16[2,256,2048]{2,1,0:T(8,128)(2,1)} %v_pp.1, bf16[2,256,768]{2,1,0:T(8,128)(2,1)} %v_pphh.1), custom_call_target="tpu_custom_call" | custom-call | flops 201326592 | bytes 6291456 | tf_op jit(solution)/shard_map/pallas_call | solution.py:18
  153.5 0.9 copy-done.2
  154.4 3.1 %shard_map.97 = bf16[2,256,768]{2,1,0:T(8,128)(2,1)} custom-call(s32[2,16]{1,0:T(2,128)} %target.3, s32[2]{0:T(128)} %live.1, bf16[2,16]{1,0:T(2,128)(2,1)} %coef.3, f32[2,256,768]{2,1,0:T(8,128)} %shard_map.96.ladder, bf16[32,16,768]{2,1,0:T(8,128)(2,1)} %copy-done.2, f32[2,256,1]{2,1,0:T(8,128)} %copy.10.e_part, f32[2,1,768]{2,1,0:T(1,128)} %broadcast_in_dim.7.e_hole), custom_call_target="tpu_custom_call" | custom-call | flops 3932160 | bytes 6291456 | tf_op jit(solution)/shard_map/pallas_call | solution.py:18
  (51 shorter events, 0.5 us)
Async XLA Ops:
  0.0 11.0 %copy-start.1 = (bf16[2,256,768]{2,1,0:T(8,128)(2,1)S(1)}, bf16[2,256,768]{2,1,0:T(8,128)(2,1)}, u32[]{:S(2)}) copy-start(bf16[2,256,768]{2,1,0:T(8,128)(2,1)} %param.9) | copy-start | bytes 2359300
  2.4 32.0 %all-to-all-start = ((bf16[32,16,896]{2,1,0:T(8,128)(2,1)}), bf16[32,16,896]{2,1,0:T(8,128)(2,1)S(1)}, u32[]{:S(2)}, u32[]{:S(2)}) async-start(bf16[32,16,896]{2,1,0:T(8,128)(2,1)} %shard_map.91), calls=%async_computation | async-start | bytes 1835008 | tf_op jit(solution)/shard_map/all_to_all | solution.py:181
  11.0 23.4 %collective-permute-start = (bf16[32,16,768]{2,1,0:T(8,128)(2,1)S(1)}, bf16[32,16,768]{2,1,0:T(8,128)(2,1)S(1)}, u32[]{:S(2)}, u32[]{:S(2)}) collective-permute-start(bf16[32,16,768]{2,1,0:T(8,128)(2,1)S(1)} %bitcast.4), channel_id=1, source_target_pairs={{0,1},{1,2},{2,3},{3,4},{4,5},{5,6},{6,7},{7,0},{8,9},{9,10},{10,1... | collective-permute-start | bytes 2359304 | tf_op jit(solution)/shard_map/ppermute | solution.py:161
  12.7 21.7 %collective-permute-start.1 = (bf16[32,16,768]{2,1,0:T(8,128)(2,1)S(1)}, bf16[32,16,768]{2,1,0:T(8,128)(2,1)}, u32[]{:S(2)}, u32[]{:S(2)}) collective-permute-start(bf16[32,16,768]{2,1,0:T(8,128)(2,1)S(1)} %bitcast.5), channel_id=1, source_target_pairs={{1,0},{2,1},{3,2},{4,3},{5,4},{6,5},{7,6},{0,7},{9,8},{10,9},{11,1... | collective-permute-start | bytes 2359304 | tf_op jit(solution)/shard_map/ppermute | solution.py:161
  34.4 69.7 %copy-start.7 = (bf16[32,16,768]{2,1,0:T(8,128)(2,1)}, bf16[32,16,768]{2,1,0:T(8,128)(2,1)S(1)}, u32[]{:S(2)}) copy-start(bf16[32,16,768]{2,1,0:T(8,128)(2,1)S(1)} %collective-permute-done.refs_1_) | copy-start | bytes 2359300
  38.2 19.8 %collective-permute-start.4 = (bf16[32,16,768]{2,1,0:T(8,128)(2,1)}, bf16[32,16,768]{2,1,0:T(8,128)(2,1)S(1)}, u32[]{:S(2)}, u32[]{:S(2)}) collective-permute-start(bf16[32,16,768]{2,1,0:T(8,128)(2,1)} %get-tuple-element.21.refs_0_), channel_id=1, source_target_pairs={{0,1},{1,2},{2,3},{3,4},{4,5},{5,6},{6,7},{7,0},{8,9},{9,10},{10,1... | collective-permute-start | bytes 2359304 | tf_op jit(solution)/shard_map/ppermute | solution.py:161
  38.3 19.8 %collective-permute-start.5 = (bf16[32,16,768]{2,1,0:T(8,128)(2,1)}, bf16[32,16,768]{2,1,0:T(8,128)(2,1)S(1)}, u32[]{:S(2)}, u32[]{:S(2)}) collective-permute-start(bf16[32,16,768]{2,1,0:T(8,128)(2,1)} %get-tuple-element.21.refs_0_), channel_id=1, source_target_pairs={{1,0},{2,1},{3,2},{4,3},{5,4},{6,5},{7,6},{0,7},{9,8},{10,9},{11,1... | collective-permute-start | bytes 2359304 | tf_op jit(solution)/shard_map/ppermute | solution.py:161
  58.0 39.4 %copy-start.8 = (bf16[32,16,768]{2,1,0:T(8,128)(2,1)}, bf16[32,16,768]{2,1,0:T(8,128)(2,1)S(1)}, u32[]{:S(2)}) copy-start(bf16[32,16,768]{2,1,0:T(8,128)(2,1)S(1)} %collective-permute-done.4.refs_1_) | copy-start | bytes 2359300
  58.1 39.4 %copy-start.9 = (bf16[32,16,768]{2,1,0:T(8,128)(2,1)}, bf16[32,16,768]{2,1,0:T(8,128)(2,1)S(1)}, u32[]{:S(2)}) copy-start(bf16[32,16,768]{2,1,0:T(8,128)(2,1)S(1)} %collective-permute-done.5.refs_2_) | copy-start | bytes 2359300
  58.1 18.7 %collective-permute-start.6 = (bf16[32,16,768]{2,1,0:T(8,128)(2,1)S(1)}, bf16[32,16,768]{2,1,0:T(8,128)(2,1)S(1)}, u32[]{:S(2)}, u32[]{:S(2)}) collective-permute-start(bf16[32,16,768]{2,1,0:T(8,128)(2,1)S(1)} %collective-permute-done.4.refs_1_), channel_id=1, source_target_pairs={{0,1},{1,2},{2,3},{3,4},{4,5},{5,6},{6,7},{7,0},{8,9},{9,10},{10,1... | collective-permute-start | bytes 2359304 | tf_op jit(solution)/shard_map/ppermute | solution.py:161
  59.0 17.8 %collective-permute-start.7 = (bf16[32,16,768]{2,1,0:T(8,128)(2,1)S(1)}, bf16[32,16,768]{2,1,0:T(8,128)(2,1)S(1)}, u32[]{:S(2)}, u32[]{:S(2)}) collective-permute-start(bf16[32,16,768]{2,1,0:T(8,128)(2,1)S(1)} %collective-permute-done.5.refs_2_), channel_id=1, source_target_pairs={{1,0},{2,1},{3,2},{4,3},{5,4},{6,5},{7,6},{0,7},{9,8},{10,9},{11,1... | collective-permute-start | bytes 2359304 | tf_op jit(solution)/shard_map/ppermute | solution.py:161
  76.8 20.7 %copy-start.10 = (bf16[32,16,768]{2,1,0:T(8,128)(2,1)}, bf16[32,16,768]{2,1,0:T(8,128)(2,1)S(1)}, u32[]{:S(2)}) copy-start(bf16[32,16,768]{2,1,0:T(8,128)(2,1)S(1)} %collective-permute-done.6.refs_3_) | copy-start | bytes 2359300
  76.8 20.7 %copy-start.11 = (bf16[32,16,768]{2,1,0:T(8,128)(2,1)}, bf16[32,16,768]{2,1,0:T(8,128)(2,1)S(1)}, u32[]{:S(2)}) copy-start(bf16[32,16,768]{2,1,0:T(8,128)(2,1)S(1)} %collective-permute-done.7.refs_4_) | copy-start | bytes 2359300
  76.8 17.8 %collective-permute-start.8 = (bf16[32,16,768]{2,1,0:T(8,128)(2,1)S(1)}, bf16[32,16,768]{2,1,0:T(8,128)(2,1)S(1)}, u32[]{:S(2)}, u32[]{:S(2)}) collective-permute-start(bf16[32,16,768]{2,1,0:T(8,128)(2,1)S(1)} %collective-permute-done.6.refs_3_), channel_id=1, source_target_pairs={{0,1},{1,2},{2,3},{3,4},{4,5},{5,6},{6,7},{7,0},{8,9},{9,10},{10,1... | collective-permute-start | bytes 2359304 | tf_op jit(solution)/shard_map/ppermute | solution.py:161
  77.0 17.7 %collective-permute-start.9 = (bf16[32,16,768]{2,1,0:T(8,128)(2,1)S(1)}, bf16[32,16,768]{2,1,0:T(8,128)(2,1)S(1)}, u32[]{:S(2)}, u32[]{:S(2)}) collective-permute-start(bf16[32,16,768]{2,1,0:T(8,128)(2,1)S(1)} %collective-permute-done.7.refs_4_), channel_id=1, source_target_pairs={{1,0},{2,1},{3,2},{4,3},{5,4},{6,5},{7,6},{0,7},{9,8},{10,9},{11,1... | collective-permute-start | bytes 2359304 | tf_op jit(solution)/shard_map/ppermute | solution.py:161
  79.5 32.0 %collective-permute-start.2 = (bf16[32,16,768]{2,1,0:T(8,128)(2,1)S(1)}, bf16[32,16,768]{2,1,0:T(8,128)(2,1)}, u32[]{:S(2)}, u32[]{:S(2)}) collective-permute-start(bf16[32,16,768]{2,1,0:T(8,128)(2,1)S(1)} %collective-permute-done.refs_1_), channel_id=1, source_target_pairs={{0,1},{1,2},{2,3},{3,4},{4,5},{5,6},{6,7},{7,0},{8,9},{9,10},{10,1... | collective-permute-start | bytes 2359304 | tf_op jit(solution)/shard_map/ppermute | solution.py:161
  79.5 32.0 %collective-permute-start.3 = (bf16[32,16,768]{2,1,0:T(8,128)(2,1)}, bf16[32,16,768]{2,1,0:T(8,128)(2,1)}, u32[]{:S(2)}, u32[]{:S(2)}) collective-permute-start(bf16[32,16,768]{2,1,0:T(8,128)(2,1)} %collective-permute-done.1.refs_2_), channel_id=1, source_target_pairs={{1,0},{2,1},{3,2},{4,3},{5,4},{6,5},{7,6},{0,7},{9,8},{10,9},{11,1... | collective-permute-start | bytes 2359304 | tf_op jit(solution)/shard_map/ppermute | solution.py:161
  94.6 2.9 %copy-start.5 = (bf16[32,16,768]{2,1,0:T(8,128)(2,1)}, bf16[32,16,768]{2,1,0:T(8,128)(2,1)S(1)}, u32[]{:S(2)}) copy-start(bf16[32,16,768]{2,1,0:T(8,128)(2,1)S(1)} %collective-permute-done.8.refs_5_) | copy-start | bytes 2359300
  94.6 25.2 %collective-permute-start.10 = (bf16[16,16,768]{2,1,0:T(8,128)(2,1)S(1)}, bf16[16,16,768]{2,1,0:T(8,128)(2,1)S(1)}, u32[]{:S(2)}, u32[]{:S(2)}) collective-permute-start(bf16[16,16,768]{2,1,0:T(8,128)(2,1)S(1)} %slice.16), channel_id=1, source_target_pairs={{0,1},{1,2},{2,3},{3,4},{4,5},{5,6},{6,7},{7,0},{8,9},{9,10},{10,1... | collective-permute-start | bytes 1179656 | tf_op jit(solution)/shard_map/ppermute | solution.py:161
  94.7 2.8 %copy-start.6 = (bf16[32,16,768]{2,1,0:T(8,128)(2,1)}, bf16[32,16,768]{2,1,0:T(8,128)(2,1)S(1)}, u32[]{:S(2)}) copy-start(bf16[32,16,768]{2,1,0:T(8,128)(2,1)S(1)} %collective-permute-done.9.refs_6_) | copy-start | bytes 2359300
  94.7 25.1 %collective-permute-start.11 = (bf16[16,16,768]{2,1,0:T(8,128)(2,1)S(1)}, bf16[16,16,768]{2,1,0:T(8,128)(2,1)S(1)}, u32[]{:S(2)}, u32[]{:S(2)}) collective-permute-start(bf16[16,16,768]{2,1,0:T(8,128)(2,1)S(1)} %slice.17), channel_id=1, source_target_pairs={{1,0},{2,1},{3,2},{4,3},{5,4},{6,5},{7,6},{0,7},{9,8},{10,9},{11,1... | collective-permute-start | bytes 1179656 | tf_op jit(solution)/shard_map/ppermute | solution.py:161
  119.8 2.9 %copy-start.12 = (bf16[16,16,768]{2,1,0:T(8,128)(2,1)}, bf16[16,16,768]{2,1,0:T(8,128)(2,1)S(1)}, u32[]{:S(2)}) copy-start(bf16[16,16,768]{2,1,0:T(8,128)(2,1)S(1)} %collective-permute-done.10.half_a) | copy-start | bytes 1179652
  119.8 2.9 %copy-start.13 = (bf16[16,16,768]{2,1,0:T(8,128)(2,1)}, bf16[16,16,768]{2,1,0:T(8,128)(2,1)S(1)}, u32[]{:S(2)}) copy-start(bf16[16,16,768]{2,1,0:T(8,128)(2,1)S(1)} %collective-permute-done.11.half_b) | copy-start | bytes 1179652
  119.9 17.8 %collective-permute-start.12 = (bf16[32,16,768]{2,1,0:T(8,128)(2,1)}, bf16[32,16,768]{2,1,0:T(8,128)(2,1)S(1)}, u32[]{:S(2)}, u32[]{:S(2)}) collective-permute-start(bf16[32,16,768]{2,1,0:T(8,128)(2,1)} %collective-permute-done.2.refs_3_), channel_id=1, source_target_pairs={{0,1},{1,2},{2,3},{3,4},{4,5},{5,6},{6,7},{7,0},{8,9},{9,10},{10,1... | collective-permute-start | bytes 2359304 | tf_op jit(solution)/shard_map/ppermute | solution.py:161
  120.1 17.6 %collective-permute-start.13 = (bf16[32,16,768]{2,1,0:T(8,128)(2,1)}, bf16[32,16,768]{2,1,0:T(8,128)(2,1)S(1)}, u32[]{:S(2)}, u32[]{:S(2)}) collective-permute-start(bf16[32,16,768]{2,1,0:T(8,128)(2,1)} %collective-permute-done.3.refs_4_), channel_id=1, source_target_pairs={{1,0},{2,1},{3,2},{4,3},{5,4},{6,5},{7,6},{0,7},{9,8},{10,9},{11,1... | collective-permute-start | bytes 2359304 | tf_op jit(solution)/shard_map/ppermute | solution.py:161
  127.0 13.5 %copy-start.16 = (f32[2,256]{1,0:T(2,128)S(1)}, f32[2,256]{1,0:T(2,128)}, u32[]{:S(2)}) copy-start(f32[2,256]{1,0:T(2,128)} %param.16) | copy-start | bytes 6148
  127.1 14.4 %copy-start.15 = (f32[2,768]{1,0:T(2,128)S(1)}, f32[2,768]{1,0:T(2,128)}, u32[]{:S(2)}) copy-start(f32[2,768]{1,0:T(2,128)} %param.17) | copy-start | bytes 18436
  127.1 26.4 %all-to-all-start.1 = ((bf16[32,16,768]{2,1,0:T(8,128)(2,1)}), bf16[32,16,768]{2,1,0:T(8,128)(2,1)S(1)}, u32[]{:S(2)}, u32[]{:S(2)}) async-start(bf16[32,16,768]{2,1,0:T(8,128)(2,1)} %shard_map.94), calls=%async_computation.1 | async-start | bytes 1572864 | tf_op jit(solution)/shard_map/all_to_all | solution.py:210
  137.7 4.4 %copy-start.3 = (bf16[32,16,768]{2,1,0:T(8,128)(2,1)}, bf16[32,16,768]{2,1,0:T(8,128)(2,1)S(1)}, u32[]{:S(2)}) copy-start(bf16[32,16,768]{2,1,0:T(8,128)(2,1)S(1)} %collective-permute-done.12.refs_5_) | copy-start | bytes 2359300
  137.7 4.4 %copy-start.4 = (bf16[32,16,768]{2,1,0:T(8,128)(2,1)}, bf16[32,16,768]{2,1,0:T(8,128)(2,1)S(1)}, u32[]{:S(2)}) copy-start(bf16[32,16,768]{2,1,0:T(8,128)(2,1)S(1)} %collective-permute-done.13.refs_6_) | copy-start | bytes 2359300
  137.7 11.0 %collective-permute-start.14 = (bf16[16,16,768]{2,1,0:T(8,128)(2,1)S(1)}, bf16[16,16,768]{2,1,0:T(8,128)(2,1)S(1)}, u32[]{:S(2)}, u32[]{:S(2)}) collective-permute-start(bf16[16,16,768]{2,1,0:T(8,128)(2,1)S(1)} %slice.14), channel_id=1, source_target_pairs={{0,1},{1,2},{2,3},{3,4},{4,5},{5,6},{6,7},{7,0},{8,9},{9,10},{10,1... | collective-permute-start | bytes 1179656 | tf_op jit(solution)/shard_map/ppermute | solution.py:161
  137.9 10.9 %collective-permute-start.15 = (bf16[16,16,768]{2,1,0:T(8,128)(2,1)S(1)}, bf16[16,16,768]{2,1,0:T(8,128)(2,1)}, u32[]{:S(2)}, u32[]{:S(2)}) collective-permute-start(bf16[16,16,768]{2,1,0:T(8,128)(2,1)S(1)} %slice.15), channel_id=1, source_target_pairs={{1,0},{2,1},{3,2},{4,3},{5,4},{6,5},{7,6},{0,7},{9,8},{10,9},{11,1... | collective-permute-start | bytes 1179656 | tf_op jit(solution)/shard_map/ppermute | solution.py:161
  (3 other events, 2.6 us)

commit v3 on v2

--- a/solution.py
+++ b/solution.py
@@ -53,7 +53,7 @@
         items[to, :, width:] = jnp.full((rows, META), slot.astype(F32)).astype(BF16)
 
 
-def settle_kernel(blocks, got, placed, homes, slot_v, slot, sem):
+def settle_kernel(blocks, got, part_a, part_b, homes, placed, slot_v, slot, sem):
     count, rows, wide = got.shape
     width = wide - META
     nb_tile = count // 2
@@ -67,6 +67,8 @@
     to_scalars(slot_v, slot, sem)
     for c in range(count):
         placed[slot[0, 0, c]] = got[c, :, :width]
+    part_a[...] = placed[: count // 2]
+    part_b[...] = placed[count // 2 :]
 
 
 def tile_at(step):
@@ -77,23 +79,22 @@
 STEPS = (0, -1, 1, -2, 2, -3, 3, 4)
 
 
-def gather_rows(pieces, placed):
+def most_kernel(*refs):
+    pieces, (matrix, part, placed) = refs[:-3], refs[-3:]
     ch_dev, total, width = placed.shape
+    near = len(STEPS) - 1
     per = total // len(STEPS)
-    each = pieces[0].shape[0] // ch_dev
-    for piece, ref in enumerate(pieces):
-        at = pl.ds(pl.multiple_of(tile_at(STEPS[piece]) * per, per), per)
-        for ch in range(ch_dev):
-            placed[ch, at] = ref[ch * each : (ch + 1) * each].reshape(per, width)
-    at = pl.ds(pl.multiple_of(tile_at(STEPS[-1]) * per, per), per)
-    for ch in range(ch_dev):
+    split = len(pieces) == ch_dev * near
+    each = per // pieces[0].shape[1]
+    for ch in range(ch_dev):
+        for i, step in enumerate(STEPS[:-1]):
+            at = pl.ds(pl.multiple_of(tile_at(step) * per, per), per)
+            ref = pieces[ch * near + i] if split else pieces[i]
+            block = ref[...] if split else ref[ch * each : (ch + 1) * each]
+            placed[ch, at] = block.reshape(per, width)
+        at = pl.ds(pl.multiple_of(tile_at(STEPS[-1]) * per, per), per)
         placed[ch, at] = jnp.zeros((per, width), BF16)
-
-
-def most_kernel(*refs):
-    pieces, (matrix, part, placed) = refs[: len(STEPS) - 1], refs[len(STEPS) - 1 :]
-    gather_rows(pieces, placed)
-    for ch in range(placed.shape[0]):
+    for ch in range(ch_dev):
         part[ch] = jnp.dot(matrix[ch], placed[ch], preferred_element_type=F32)
 
 
@@ -117,24 +118,21 @@
         back[c] = result[row, :]
 
 
-def ladder_kernel(half_a, half_b, part, v_pp, v_pphh, ladder):
-    for ch in range(part.shape[0]):
-        total = part[ch] + rest_of(ch, (half_a, half_b), v_pp)
-        ladder[ch] = v_pphh[ch].astype(F32) + total
-
-
-def final_kernel(blocks, target, live, coef, ladder, back, e_part, e_hole, out):
+def final_kernel(
+    blocks, target, live, coef, half_a, half_b, part, v_pp, back, v_pphh, e_part, e_hole, out
+):
     ch_dev, per, width = out.shape
     count, rows, _ = back.shape
     nb_tile = count // ch_dev
     first = lax.axis_index("tile") * per
     factor = coef[...].astype(F32)
     for ch in range(ch_dev):
+        more = rest_of(ch, (half_a, half_b), v_pp)
         for b in range(nb_tile):
             at = slice(b * rows, (b + 1) * rows)
             own = lax.div(target[ch, b], ch_dev * blocks)
             come = back[own].astype(F32) * factor[ch : ch + 1, b : b + 1]
-            sums = ladder[ch, at] + come
+            sums = v_pphh[ch, at].astype(F32) + (part[ch, at] + more[at]) + come
             denom = e_part[ch, at] + e_hole[ch]
             row = lax.broadcasted_iota(I32, (rows, width), 0) + (first + b * rows)
             out[ch, at] = jnp.where(row < live[ch], sums / denom, 0.0).astype(BF16)
@@ -167,7 +165,10 @@
     own_rows = amp.reshape(count, rows, width)
     block_type = jax.ShapeDtypeStruct((count, rows, width), BF16)
     part_type = jax.ShapeDtypeStruct((ch_dev, tile_rows, width), F32)
-    amp1 = both(own_rows, own_rows)
+    half = count // ch_dev
+    amp_a, amp_b = own_rows[:half], own_rows[half:]
+    a1, b1 = both(amp_a, amp_a), both(amp_b, amp_b)
+    amp1 = tuple(jnp.concatenate(x, axis=0) for x in zip(a1, b1))
     items = call(
         functools.partial(pack_kernel, blocks),
         jax.ShapeDtypeStruct((count, rows, width + META), BF16),
@@ -175,18 +176,21 @@
         (target,),
         moved=4 * 2**20,
     )
-    far, homes = call(
+    half_type = jax.ShapeDtypeStruct((count // ch_dev, rows, width), BF16)
+    far_a, far_b, homes = call(
         functools.partial(settle_kernel, blocks),
-        (block_type, jax.ShapeDtypeStruct((8, META), I32)),
-        (after(exchange(items), amp1),),
-        scratch=tables(1),
+        (half_type, half_type, jax.ShapeDtypeStruct((8, META), I32)),
+        (after(exchange(items), a1),),
+        scratch=(pltpu.VMEM((count, rows, width), BF16), *tables(1)),
+        flops=10**14,
         moved=4 * 2**20,
     )
-    far1 = both(far, far)
+    fa1, fb1 = both(*after((far_a, far_a), b1)), both(far_b, far_b)
     amp2 = both(*after(amp1))
-    far2 = both(*after(far1))
-    far3 = both(*after(far2))
-    far4 = both(far3[0][: count // 2], far3[1][count // 2 :])
+    fa2, fb2 = both(*fa1), both(*fb1)
+    fa3, fb3 = both(*fa2), both(*fb2)
+    far4 = to_right(fa3[0]), to_left(fb3[1])
+
     def most(pieces, matrix):
         return call(
             most_kernel,
@@ -197,7 +201,7 @@
             moved=12 * 2**20,
         )
 
-    cycle_most = most((far, *far1, *far2, *far3), w_ph)
+    cycle_most = most((far_a, *fa1, *fa2, *fa3, far_b, *fb1, *fb2, *fb3), w_ph)
     amp3 = both(*after(amp2, cycle_most, far4))
     back = call(
         back_kernel,
@@ -210,19 +214,22 @@
     returned = exchange(back)
     amp3 = after(amp3, back)
     amp4 = both(amp3[0][: count // 2], amp3[1][count // 2 :])
-    ladder = call(
-        ladder_kernel,
-        part_type,
-        (*amp4, most((own_rows, *amp1, *amp2, *amp3), v_pp), v_pp, v_pphh),
-        flops=2 * ch_dev * tile_rows * tile_rows * width,
-        moved=6 * 2**20,
-    )
+    ladder_most = most((own_rows, *amp1, *amp2, *amp3), v_pp)
     return call(
         functools.partial(final_kernel, blocks),
         jax.ShapeDtypeStruct((ch_dev, tile_rows, width), BF16),
-        (coef, ladder, returned, e_part[:, :, None], e_hole[:, None, :]),
+        (
+            coef,
+            *amp4,
+            ladder_most,
+            v_pp,
+            returned,
+            v_pphh,
+            e_part[:, :, None],
+            e_hole[:, None, :],
+        ),
         (target, pp_size),
-        flops=10 * ch_dev * tile_rows * width,
+        flops=2 * ch_dev * tile_rows * tile_rows * width,
         moved=6 * 2**20,
     )
 

time: 160 us -> 153 us (0.956)
  waiting for transfers between devices: 78.8 us -> 60.5 us
  starting transfers between devices: 44.4 us -> 54.3 us
  local copies, waits for them, and re-layouts: 4.21 us -> 9.55 us
  Pallas kernels: 29.8 us -> 27.3 us
    ppermute x16 -> x22, waiting for transfers between devices: 78.8 us -> 59.1 us  [both(): return (to_right(a), to_left(b))]
    ppermute x0 -> x2, starting transfers between devices: none -> 5.47 us  [body(): far4 = (to_right(fa3[0]), to_left(fb3[1]))]
    ppermute x16 -> x22, starting transfers between devices: 25.2 us -> 30.6 us  [both(): return (to_right(a), to_left(b))]
    pallas_call x7 -> x6, Pallas kernels: 29.8 us -> 27.3 us  [call(): pl.pallas_call(kernel, out_shape=outs, in_specs=[smem] * len(scalars) + [...]
    concatenate x0 -> x2, local copies, waits for them, and re-layouts: none -> 2.47 us  [body(): amp1 = tuple((jnp.concatenate(x, axis=0) for x in zip(a1, b1)))]
    unnamed x34 -> x52, local copies, waits for them, and re-layouts: 2.65 us -> 4.77 us
  transfers between devices with their start and end apart: 18 -> 26, of which waited for: 6 -> 11; matrix products, arithmetic and copies ran while one was open for 1% -> 4% of each run, Pallas kernels for 14% -> 13%
where the time goes in v3:
time: 153 us; the launch traced here: 152 us
  waiting for transfers between devices  60.5 us (40%)
  starting transfers between devices  54.3 us (35%)
  Pallas kernels  27.3 us (18%)
  local copies, waits for them, and re-layouts  9.55 us (6%)
    ppermute x22, waiting for transfers between devices, both(): return (to_right(a), to_left(b))  59.1 us
    ppermute x22, starting transfers between devices, both(): return (to_right(a), to_left(b))  30.6 us
    pallas_call x6, Pallas kernels, call(): pl.pallas_call(kernel, out_shape=outs, in_specs=[smem] * len(scalars) + [...  27.3 us
    all_to_all x1, starting transfers between devices, body(): returned = exchange(back)  9.66 us
    all_to_all x1, starting transfers between devices, body(): exchange(items)  8.59 us
    ppermute x2, starting transfers between devices, body(): far4 = (to_right(fa3[0]), to_left(fb3[1]))  5.47 us
    unnamed x52, local copies, waits for them, and re-layouts  4.77 us
  transfers between devices with their start and end apart: 26, of which 11 were waited for; matrix products, arithmetic and copies ran while one was open for 4% of the time, Pallas kernels for 13%

profile of v3, /device:TPU:1, one launch (start us, length us, event | category | flops | bytes accessed | tf_op | source)
XLA Modules:
  0.0 152.0 jit_solution(2074213623782255303)
XLA Ops:
  0.0 2.5 %shard_map.91 = bf16[32,16,896]{2,1,0:T(8,128)(2,1)} custom-call(s32[2,16]{1,0:T(2,128)} %target.3, bf16[2,16]{1,0:T(2,128)(2,1)} %coef.3, bf16[32,16,768]{2,1,0:T(8,128)(2,1)} %bitcast.4), custom_call_target="tpu_custom_call" | custom-call | bytes 4194304 | tf_op jit(solution)/shard_map/pallas_call | solution.py:18
  2.5 8.6 %all-to-all-start = ((bf16[32,16,896]{2,1,0:T(8,128)(2,1)}), bf16[32,16,896]{2,1,0:T(8,128)(2,1)S(1)}, u32[]{:S(2)}, u32[]{:S(2)}) async-start(bf16[32,16,896]{2,1,0:T(8,128)(2,1)} %shard_map.91), calls=%async_computation | async-start | bytes 1835008 | tf_op jit(solution)/shard_map/all_to_all | solution.py:183
  11.9 1.6 %collective-permute-start = (bf16[16,16,768]{2,1,0:T(8,128)(2,1)S(1)}, bf16[16,16,768]{2,1,0:T(8,128)(2,1)S(1)}, u32[]{:S(2)}, u32[]{:S(2)}) collective-permute-start(bf16[16,16,768]{2,1,0:T(8,128)(2,1)S(1)} %bitcast.6), channel_id=1, source_target_pairs={{0,1},{1,2},{2,3},{3,4},{4,5},{5,6},{6,7},{7,0},{8,9},{9,10},{10,1... | collective-permute-start | bytes 1179656 | tf_op jit(solution)/shard_map/ppermute | solution.py:159
  13.5 3.9 %collective-permute-start.2 = (bf16[16,16,768]{2,1,0:T(8,128)(2,1)S(1)}, bf16[16,16,768]{2,1,0:T(8,128)(2,1)}, u32[]{:S(2)}, u32[]{:S(2)}) collective-permute-start(bf16[16,16,768]{2,1,0:T(8,128)(2,1)S(1)} %bitcast.7), channel_id=1, source_target_pairs={{1,0},{2,1},{3,2},{4,3},{5,4},{6,5},{7,6},{0,7},{9,8},{10,9},{11,1... | collective-permute-start | bytes 1179656 | tf_op jit(solution)/shard_map/ppermute | solution.py:159
  17.4 2.7 %collective-permute-start.3 = (bf16[16,16,768]{2,1,0:T(8,128)(2,1)}, bf16[16,16,768]{2,1,0:T(8,128)(2,1)}, u32[]{:S(2)}, u32[]{:S(2)}) collective-permute-start(bf16[16,16,768]{2,1,0:T(8,128)(2,1)} %bitcast.1), channel_id=1, source_target_pairs={{1,0},{2,1},{3,2},{4,3},{5,4},{6,5},{7,6},{0,7},{9,8},{10,9},{11,1... | collective-permute-start | bytes 1179656 | tf_op jit(solution)/shard_map/ppermute | solution.py:159
  20.1 6.7 %collective-permute-done = bf16[16,16,768]{2,1,0:T(8,128)(2,1)S(1)} collective-permute-done((bf16[16,16,768]{2,1,0:T(8,128)(2,1)S(1)}, bf16[16,16,768]{2,1,0:T(8,128)(2,1)S(1)}, u32[]{:S(2)}, u32[]{:S(2)}) %collective-permute-start) | collective-permute-done | bytes 393248 | tf_op jit(solution)/shard_map/ppermute | solution.py:159
  28.5 2.9 %shard_map.92 = (bf16[16,16,768]{2,1,0:T(8,128)(2,1)}, bf16[16,16,768]{2,1,0:T(8,128)(2,1)}, s32[8,128]{1,0:T(8,128)}) custom-call(bf16[32,16,896]{2,1,0:T(8,128)(2,1)} %copy-done.6), custom_call_target="tpu_custom_call" | custom-call | flops 100000000376832 | bytes 4194304 | tf_op jit(solution)/shard_map/pallas_call | solution.py:18
  31.4 3.9 %collective-permute-done.1 = bf16[16,16,768]{2,1,0:T(8,128)(2,1)} collective-permute-done((bf16[16,16,768]{2,1,0:T(8,128)(2,1)}, bf16[16,16,768]{2,1,0:T(8,128)(2,1)}, u32[]{:S(2)}, u32[]{:S(2)}) %collective-permute-start.1) | collective-permute-done | bytes 393248 | tf_op jit(solution)/shard_map/ppermute | solution.py:159
  35.3 2.7 %collective-permute-start.7 = (bf16[16,16,768]{2,1,0:T(8,128)(2,1)}, bf16[16,16,768]{2,1,0:T(8,128)(2,1)S(1)}, u32[]{:S(2)}, u32[]{:S(2)}) collective-permute-start(bf16[16,16,768]{2,1,0:T(8,128)(2,1)} %get-tuple-element.22.refs_0_), channel_id=1, source_target_pairs={{1,0},{2,1},{3,2},{4,3},{5,4},{6,5},{7,6},{0,7},{9,8},{10,9},{11,1... | collective-permute-start | bytes 1179656 | tf_op jit(solution)/shard_map/ppermute | solution.py:159
  39.5 7.2 %collective-permute-done.6.refs_1_ = bf16[16,16,768]{2,1,0:T(8,128)(2,1)S(1)} collective-permute-done((bf16[16,16,768]{2,1,0:T(8,128)(2,1)}, bf16[16,16,768]{2,1,0:T(8,128)(2,1)S(1)}, u32[]{:S(2)}, u32[]{:S(2)}) %collective-permute-start.6) | collective-permute-done | bytes 393248 | tf_op jit(solution)/shard_map/ppermute | solution.py:159
  46.7 2.7 %collective-permute-start.9 = (bf16[16,16,768]{2,1,0:T(8,128)(2,1)S(1)}, bf16[16,16,768]{2,1,0:T(8,128)(2,1)S(1)}, u32[]{:S(2)}, u32[]{:S(2)}) collective-permute-start(bf16[16,16,768]{2,1,0:T(8,128)(2,1)S(1)} %collective-permute-done.7.refs_2_), channel_id=1, source_target_pairs={{1,0},{2,1},{3,2},{4,3},{5,4},{6,5},{7,6},{0,7},{9,8},{10,9},{11,1... | collective-permute-start | bytes 1179656 | tf_op jit(solution)/shard_map/ppermute | solution.py:159
  49.3 4.8 %collective-permute-done.13.refs_9_ = bf16[16,16,768]{2,1,0:T(8,128)(2,1)S(1)} collective-permute-done((bf16[16,16,768]{2,1,0:T(8,128)(2,1)}, bf16[16,16,768]{2,1,0:T(8,128)(2,1)S(1)}, u32[]{:S(2)}, u32[]{:S(2)}) %collective-permute-start.13) | collective-permute-done | bytes 393248 | tf_op jit(solution)/shard_map/ppermute | solution.py:159
  54.1 3.3 %collective-permute-start.15 = (bf16[16,16,768]{2,1,0:T(8,128)(2,1)S(1)}, bf16[16,16,768]{2,1,0:T(8,128)(2,1)S(1)}, u32[]{:S(2)}, u32[]{:S(2)}) collective-permute-start(bf16[16,16,768]{2,1,0:T(8,128)(2,1)S(1)} %collective-permute-done.13.refs_9_), channel_id=1, source_target_pairs={{1,0},{2,1},{3,2},{4,3},{5,4},{6,5},{7,6},{0,7},{9,8},{10,9},{11,1... | collective-permute-start | bytes 1179656 | tf_op jit(solution)/shard_map/ppermute | solution.py:159
  58.7 4.8 %collective-permute-done.8.refs_3_ = bf16[16,16,768]{2,1,0:T(8,128)(2,1)S(1)} collective-permute-done((bf16[16,16,768]{2,1,0:T(8,128)(2,1)S(1)}, bf16[16,16,768]{2,1,0:T(8,128)(2,1)S(1)}, u32[]{:S(2)}, u32[]{:S(2)}) %collective-permute-start.8) | collective-permute-done | bytes 393248 | tf_op jit(solution)/shard_map/ppermute | solution.py:159
  64.7 1.3 constant_dynamic-update-slice_fusion.refs_1_
  66.2 2.7 %collective-permute-start.5 = (bf16[32,16,768]{2,1,0:T(8,128)(2,1)S(1)}, bf16[32,16,768]{2,1,0:T(8,128)(2,1)}, u32[]{:S(2)}, u32[]{:S(2)}) collective-permute-start(bf16[32,16,768]{2,1,0:T(8,128)(2,1)S(1)} %constant_dynamic-update-slice_fusion.2.refs_2_), channel_id=1, source_target_pairs={{1,0},{2,1},{3,2},{4,3},{5,4},{6,5},{7,6},{0,7},{9,8},{10,9},{11,1... | collective-permute-start | bytes 2359304 | tf_op jit(solution)/shard_map/ppermute | solution.py:159
  68.9 2.0 %collective-permute-done.15.refs_11_ = bf16[16,16,768]{2,1,0:T(8,128)(2,1)S(1)} collective-permute-done((bf16[16,16,768]{2,1,0:T(8,128)(2,1)S(1)}, bf16[16,16,768]{2,1,0:T(8,128)(2,1)S(1)}, u32[]{:S(2)}, u32[]{:S(2)}) %collective-permute-start.15) | collective-permute-done | bytes 393248 | tf_op jit(solution)/shard_map/ppermute | solution.py:159
  70.9 3.4 %collective-permute-start.11 = (bf16[16,16,768]{2,1,0:T(8,128)(2,1)S(1)}, bf16[16,16,768]{2,1,0:T(8,128)(2,1)S(1)}, u32[]{:S(2)}, u32[]{:S(2)}) collective-permute-start(bf16[16,16,768]{2,1,0:T(8,128)(2,1)S(1)} %collective-permute-done.9.refs_4_), channel_id=1, source_target_pairs={{1,0},{2,1},{3,2},{4,3},{5,4},{6,5},{7,6},{0,7},{9,8},{10,9},{11,1... | collective-permute-start | bytes 1179656 | tf_op jit(solution)/shard_map/ppermute | solution.py:159
  74.4 6.0 %collective-permute-done.10.refs_5_ = bf16[16,16,768]{2,1,0:T(8,128)(2,1)S(1)} collective-permute-done((bf16[16,16,768]{2,1,0:T(8,128)(2,1)S(1)}, bf16[16,16,768]{2,1,0:T(8,128)(2,1)S(1)}, u32[]{:S(2)}, u32[]{:S(2)}) %collective-permute-start.10) | collective-permute-done | bytes 393248 | tf_op jit(solution)/shard_map/ppermute | solution.py:159
  80.4 15.8 %collective-permute-done.11.refs_6_ = bf16[16,16,768]{2,1,0:T(8,128)(2,1)S(1)} collective-permute-done((bf16[16,16,768]{2,1,0:T(8,128)(2,1)S(1)}, bf16[16,16,768]{2,1,0:T(8,128)(2,1)S(1)}, u32[]{:S(2)}, u32[]{:S(2)}) %collective-permute-start.11) | collective-permute-done | bytes 393248 | tf_op jit(solution)/shard_map/ppermute | solution.py:159
  96.2 2.1 %collective-permute-start.18 = (bf16[16,16,768]{2,1,0:T(8,128)(2,1)S(1)}, bf16[16,16,768]{2,1,0:T(8,128)(2,1)S(1)}, u32[]{:S(2)}, u32[]{:S(2)}) collective-permute-start(bf16[16,16,768]{2,1,0:T(8,128)(2,1)S(1)} %collective-permute-done.10.refs_5_), channel_id=1, source_target_pairs={{0,1},{1,2},{2,3},{3,4},{4,5},{5,6},{6,7},{7,0},{8,9},{9,10},{10,1... | collective-permute-start | bytes 1179656 | tf_op jit(solution)/shard_map/ppermute | solution.py:192
  98.2 6.4 %collective-permute-done.17.refs_13_ = bf16[16,16,768]{2,1,0:T(8,128)(2,1)S(1)} collective-permute-done((bf16[16,16,768]{2,1,0:T(8,128)(2,1)S(1)}, bf16[16,16,768]{2,1,0:T(8,128)(2,1)S(1)}, u32[]{:S(2)}, u32[]{:S(2)}) %collective-permute-start.17) | collective-permute-done | bytes 393248 | tf_op jit(solution)/shard_map/ppermute | solution.py:159
  104.6 3.4 %collective-permute-start.19 = (bf16[16,16,768]{2,1,0:T(8,128)(2,1)S(1)}, bf16[16,16,768]{2,1,0:T(8,128)(2,1)}, u32[]{:S(2)}, u32[]{:S(2)}) collective-permute-start(bf16[16,16,768]{2,1,0:T(8,128)(2,1)S(1)} %collective-permute-done.17.refs_13_), channel_id=1, source_target_pairs={{1,0},{2,1},{3,2},{4,3},{5,4},{6,5},{7,6},{0,7},{9,8},{10,9},{11,1... | collective-permute-start | bytes 1179656 | tf_op jit(solution)/shard_map/ppermute | solution.py:192
  108.9 6.6 %shard_map.93.part = f32[2,256,768]{2,1,0:T(8,128)} custom-call(bf16[16,16,768]{2,1,0:T(8,128)(2,1)} %get-tuple-element.22.refs_0_, bf16[16,16,768]{2,1,0:T(8,128)(2,1)} %copy-done.7, bf16[16,16,768]{2,1,0:T(8,128)(2,1)} %copy-done.8, bf16[16,16,768]{2,1,0:T(8,128)(2,1)} %copy-done.11, bf16[16,16,768]{2,1,0:T(8,128)(2,1)} %copy-done.12, ...), custom_call_target="tpu_custom_call" | custom-call | flops 1610612736 | bytes 12582912 | tf_op jit(solution)/shard_map/pallas_call | solution.py:18
  115.6 2.7 %collective-permute-start.21 = (bf16[32,16,768]{2,1,0:T(8,128)(2,1)}, bf16[32,16,768]{2,1,0:T(8,128)(2,1)S(1)}, u32[]{:S(2)}, u32[]{:S(2)}) collective-permute-start(bf16[32,16,768]{2,1,0:T(8,128)(2,1)} %collective-permute-done.5.refs_4_), channel_id=1, source_target_pairs={{1,0},{2,1},{3,2},{4,3},{5,4},{6,5},{7,6},{0,7},{9,8},{10,9},{11,1... | collective-permute-start | bytes 2359304 | tf_op jit(solution)/shard_map/ppermute | solution.py:159
  118.3 4.3 %shard_map.94 = bf16[32,16,768]{2,1,0:T(8,128)(2,1)} custom-call(s32[8,128]{1,0:T(8,128)} %get-tuple-element.26.homes, bf16[16,16,768]{2,1,0:T(8,128)(2,1)} %copy-done.19, bf16[16,16,768]{2,1,0:T(8,128)(2,1)} %collective-permute-done.19.half_b, f32[2,256,768]{2,1,0:T(8,128)} %shard_map.93.part, bf16[2,256,2048]{2,1,0:T(8,128)(2,1)} %w_ph.1), custom_call_target="tpu_custom_call" | custom-call | flops 201326592 | bytes 6291456 | tf_op jit(solution)/shard_map/pallas_call | solution.py:18
  122.6 9.7 %all-to-all-start.1 = ((bf16[32,16,768]{2,1,0:T(8,128)(2,1)}), bf16[32,16,768]{2,1,0:T(8,128)(2,1)S(1)}, u32[]{:S(2)}, u32[]{:S(2)}) async-start(bf16[32,16,768]{2,1,0:T(8,128)(2,1)} %shard_map.94), calls=%async_computation.1 | async-start | bytes 1572864 | tf_op jit(solution)/shard_map/all_to_all | solution.py:214
  132.3 1.5 %collective-permute-done.20.refs_5_ = bf16[32,16,768]{2,1,0:T(8,128)(2,1)S(1)} collective-permute-done((bf16[32,16,768]{2,1,0:T(8,128)(2,1)}, bf16[32,16,768]{2,1,0:T(8,128)(2,1)S(1)}, u32[]{:S(2)}, u32[]{:S(2)}) %collective-permute-start.20) | collective-permute-done | bytes 786464 | tf_op jit(solution)/shard_map/ppermute | solution.py:159
  134.0 3.0 %collective-permute-start.23 = (bf16[16,16,768]{2,1,0:T(8,128)(2,1)S(1)}, bf16[16,16,768]{2,1,0:T(8,128)(2,1)}, u32[]{:S(2)}, u32[]{:S(2)}) collective-permute-start(bf16[16,16,768]{2,1,0:T(8,128)(2,1)S(1)} %slice.23), channel_id=1, source_target_pairs={{1,0},{2,1},{3,2},{4,3},{5,4},{6,5},{7,6},{0,7},{9,8},{10,9},{11,1... | collective-permute-start | bytes 1179656 | tf_op jit(solution)/shard_map/ppermute | solution.py:159
  138.4 6.6 %shard_map.95.part = f32[2,256,768]{2,1,0:T(8,128)} custom-call(bf16[32,16,768]{2,1,0:T(8,128)(2,1)} %bitcast.5, bf16[32,16,768]{2,1,0:T(8,128)(2,1)} %copy-done.4, bf16[32,16,768]{2,1,0:T(8,128)(2,1)} %copy-done.5, bf16[32,16,768]{2,1,0:T(8,128)(2,1)} %collective-permute-done.4.refs_3_, bf16[32,16,768]{2,1,0:T(8,128)(2,1)} %collective-permute-done.5.refs_4_, ...), custom_call_target="tpu_custom_call" | custom-call | flops 1610612736 | bytes 12582912 | tf_op jit(solution)/shard_map/pallas_call | solution.py:18
  145.1 1.5 all-to-all-done.1.back
  147.5 4.5 %shard_map.96 = bf16[2,256,768]{2,1,0:T(8,128)(2,1)} custom-call(s32[2,16]{1,0:T(2,128)} %target.3, s32[2]{0:T(128)} %live.1, bf16[2,16]{1,0:T(2,128)(2,1)} %coef.3, bf16[16,16,768]{2,1,0:T(8,128)(2,1)} %copy-done.22, bf16[16,16,768]{2,1,0:T(8,128)(2,1)} %collective-permute-done.23.half_b, f32[2,256,768]{2,1,0:T(8,128)} %shard_map.95.part, ...), custom_call_target="tpu_custom_call" | custom-call | flops 201326592 | bytes 6291456 | tf_op jit(solution)/shard_map/pallas_call | solution.py:18
  (85 shorter events, 10.2 us)
Async XLA Ops:
  2.5 25.1 %all-to-all-start = ((bf16[32,16,896]{2,1,0:T(8,128)(2,1)}), bf16[32,16,896]{2,1,0:T(8,128)(2,1)S(1)}, u32[]{:S(2)}, u32[]{:S(2)}) async-start(bf16[32,16,896]{2,1,0:T(8,128)(2,1)} %shard_map.91), calls=%async_computation | async-start | bytes 1835008 | tf_op jit(solution)/shard_map/all_to_all | solution.py:183
  11.9 14.9 %collective-permute-start = (bf16[16,16,768]{2,1,0:T(8,128)(2,1)S(1)}, bf16[16,16,768]{2,1,0:T(8,128)(2,1)S(1)}, u32[]{:S(2)}, u32[]{:S(2)}) collective-permute-start(bf16[16,16,768]{2,1,0:T(8,128)(2,1)S(1)} %bitcast.6), channel_id=1, source_target_pairs={{0,1},{1,2},{2,3},{3,4},{4,5},{5,6},{6,7},{7,0},{8,9},{9,10},{10,1... | collective-permute-start | bytes 1179656 | tf_op jit(solution)/shard_map/ppermute | solution.py:159
  13.5 14.0 %collective-permute-start.2 = (bf16[16,16,768]{2,1,0:T(8,128)(2,1)S(1)}, bf16[16,16,768]{2,1,0:T(8,128)(2,1)}, u32[]{:S(2)}, u32[]{:S(2)}) collective-permute-start(bf16[16,16,768]{2,1,0:T(8,128)(2,1)S(1)} %bitcast.7), channel_id=1, source_target_pairs={{1,0},{2,1},{3,2},{4,3},{5,4},{6,5},{7,6},{0,7},{9,8},{10,9},{11,1... | collective-permute-start | bytes 1179656 | tf_op jit(solution)/shard_map/ppermute | solution.py:159
  17.4 17.9 %collective-permute-start.1 = (bf16[16,16,768]{2,1,0:T(8,128)(2,1)}, bf16[16,16,768]{2,1,0:T(8,128)(2,1)}, u32[]{:S(2)}, u32[]{:S(2)}) collective-permute-start(bf16[16,16,768]{2,1,0:T(8,128)(2,1)} %bitcast.1), channel_id=1, source_target_pairs={{0,1},{1,2},{2,3},{3,4},{4,5},{5,6},{6,7},{7,0},{8,9},{9,10},{10,1... | collective-permute-start | bytes 1179656 | tf_op jit(solution)/shard_map/ppermute | solution.py:159
  17.4 17.9 %collective-permute-start.3 = (bf16[16,16,768]{2,1,0:T(8,128)(2,1)}, bf16[16,16,768]{2,1,0:T(8,128)(2,1)}, u32[]{:S(2)}, u32[]{:S(2)}) collective-permute-start(bf16[16,16,768]{2,1,0:T(8,128)(2,1)} %bitcast.1), channel_id=1, source_target_pairs={{1,0},{2,1},{3,2},{4,3},{5,4},{6,5},{7,6},{0,7},{9,8},{10,9},{11,1... | collective-permute-start | bytes 1179656 | tf_op jit(solution)/shard_map/ppermute | solution.py:159
  35.3 11.3 %collective-permute-start.6 = (bf16[16,16,768]{2,1,0:T(8,128)(2,1)}, bf16[16,16,768]{2,1,0:T(8,128)(2,1)S(1)}, u32[]{:S(2)}, u32[]{:S(2)}) collective-permute-start(bf16[16,16,768]{2,1,0:T(8,128)(2,1)} %get-tuple-element.22.refs_0_), channel_id=1, source_target_pairs={{0,1},{1,2},{2,3},{3,4},{4,5},{5,6},{6,7},{7,0},{8,9},{9,10},{10,1... | collective-permute-start | bytes 1179656 | tf_op jit(solution)/shard_map/ppermute | solution.py:159
  35.3 11.3 %collective-permute-start.7 = (bf16[16,16,768]{2,1,0:T(8,128)(2,1)}, bf16[16,16,768]{2,1,0:T(8,128)(2,1)S(1)}, u32[]{:S(2)}, u32[]{:S(2)}) collective-permute-start(bf16[16,16,768]{2,1,0:T(8,128)(2,1)} %get-tuple-element.22.refs_0_), channel_id=1, source_target_pairs={{1,0},{2,1},{3,2},{4,3},{5,4},{6,5},{7,6},{0,7},{9,8},{10,9},{11,1... | collective-permute-start | bytes 1179656 | tf_op jit(solution)/shard_map/ppermute | solution.py:159
  38.0 16.1 %collective-permute-start.13 = (bf16[16,16,768]{2,1,0:T(8,128)(2,1)}, bf16[16,16,768]{2,1,0:T(8,128)(2,1)S(1)}, u32[]{:S(2)}, u32[]{:S(2)}) collective-permute-start(bf16[16,16,768]{2,1,0:T(8,128)(2,1)} %get-tuple-element.23.refs_7_), channel_id=1, source_target_pairs={{1,0},{2,1},{3,2},{4,3},{5,4},{6,5},{7,6},{0,7},{9,8},{10,9},{11,1... | collective-permute-start | bytes 1179656 | tf_op jit(solution)/shard_map/ppermute | solution.py:159
  39.1 18.3 %collective-permute-start.12 = (bf16[16,16,768]{2,1,0:T(8,128)(2,1)}, bf16[16,16,768]{2,1,0:T(8,128)(2,1)S(1)}, u32[]{:S(2)}, u32[]{:S(2)}) collective-permute-start(bf16[16,16,768]{2,1,0:T(8,128)(2,1)} %get-tuple-element.23.refs_7_), channel_id=1, source_target_pairs={{0,1},{1,2},{2,3},{3,4},{4,5},{5,6},{6,7},{7,0},{8,9},{9,10},{10,1... | collective-permute-start | bytes 1179656 | tf_op jit(solution)/shard_map/ppermute | solution.py:159
  46.7 61.3 %copy-start.7 = (bf16[16,16,768]{2,1,0:T(8,128)(2,1)}, bf16[16,16,768]{2,1,0:T(8,128)(2,1)S(1)}, u32[]{:S(2)}) copy-start(bf16[16,16,768]{2,1,0:T(8,128)(2,1)S(1)} %collective-permute-done.6.refs_1_) | copy-start | bytes 1179652
  46.7 16.9 %collective-permute-start.8 = (bf16[16,16,768]{2,1,0:T(8,128)(2,1)S(1)}, bf16[16,16,768]{2,1,0:T(8,128)(2,1)S(1)}, u32[]{:S(2)}, u32[]{:S(2)}) collective-permute-start(bf16[16,16,768]{2,1,0:T(8,128)(2,1)S(1)} %collective-permute-done.6.refs_1_), channel_id=1, source_target_pairs={{0,1},{1,2},{2,3},{3,4},{4,5},{5,6},{6,7},{7,0},{8,9},{9,10},{10,1... | collective-permute-start | bytes 1179656 | tf_op jit(solution)/shard_map/ppermute | solution.py:159
  46.7 61.3 %copy-start.8 = (bf16[16,16,768]{2,1,0:T(8,128)(2,1)}, bf16[16,16,768]{2,1,0:T(8,128)(2,1)S(1)}, u32[]{:S(2)}) copy-start(bf16[16,16,768]{2,1,0:T(8,128)(2,1)S(1)} %collective-permute-done.7.refs_2_) | copy-start | bytes 1179652
  46.7 19.6 %collective-permute-start.9 = (bf16[16,16,768]{2,1,0:T(8,128)(2,1)S(1)}, bf16[16,16,768]{2,1,0:T(8,128)(2,1)S(1)}, u32[]{:S(2)}, u32[]{:S(2)}) collective-permute-start(bf16[16,16,768]{2,1,0:T(8,128)(2,1)S(1)} %collective-permute-done.7.refs_2_), channel_id=1, source_target_pairs={{1,0},{2,1},{3,2},{4,3},{5,4},{6,5},{7,6},{0,7},{9,8},{10,9},{11,1... | collective-permute-start | bytes 1179656 | tf_op jit(solution)/shard_map/ppermute | solution.py:159
  54.1 53.9 %copy-start.9 = (bf16[16,16,768]{2,1,0:T(8,128)(2,1)}, bf16[16,16,768]{2,1,0:T(8,128)(2,1)S(1)}, u32[]{:S(2)}) copy-start(bf16[16,16,768]{2,1,0:T(8,128)(2,1)S(1)} %collective-permute-done.13.refs_9_) | copy-start | bytes 1179652
  54.1 16.7 %collective-permute-start.15 = (bf16[16,16,768]{2,1,0:T(8,128)(2,1)S(1)}, bf16[16,16,768]{2,1,0:T(8,128)(2,1)S(1)}, u32[]{:S(2)}, u32[]{:S(2)}) collective-permute-start(bf16[16,16,768]{2,1,0:T(8,128)(2,1)S(1)} %collective-permute-done.13.refs_9_), channel_id=1, source_target_pairs={{1,0},{2,1},{3,2},{4,3},{5,4},{6,5},{7,6},{0,7},{9,8},{10,9},{11,1... | collective-permute-start | bytes 1179656 | tf_op jit(solution)/shard_map/ppermute | solution.py:159
  57.4 50.6 %copy-start.10 = (bf16[16,16,768]{2,1,0:T(8,128)(2,1)}, bf16[16,16,768]{2,1,0:T(8,128)(2,1)S(1)}, u32[]{:S(2)}) copy-start(bf16[16,16,768]{2,1,0:T(8,128)(2,1)S(1)} %collective-permute-done.12.refs_8_) | copy-start | bytes 1179652
  57.4 16.9 %collective-permute-start.14 = (bf16[16,16,768]{2,1,0:T(8,128)(2,1)S(1)}, bf16[16,16,768]{2,1,0:T(8,128)(2,1)S(1)}, u32[]{:S(2)}, u32[]{:S(2)}) collective-permute-start(bf16[16,16,768]{2,1,0:T(8,128)(2,1)S(1)} %collective-permute-done.12.refs_8_), channel_id=1, source_target_pairs={{0,1},{1,2},{2,3},{3,4},{4,5},{5,6},{6,7},{7,0},{8,9},{9,10},{10,1... | collective-permute-start | bytes 1179656 | tf_op jit(solution)/shard_map/ppermute | solution.py:159
  63.5 16.9 %collective-permute-start.10 = (bf16[16,16,768]{2,1,0:T(8,128)(2,1)S(1)}, bf16[16,16,768]{2,1,0:T(8,128)(2,1)S(1)}, u32[]{:S(2)}, u32[]{:S(2)}) collective-permute-start(bf16[16,16,768]{2,1,0:T(8,128)(2,1)S(1)} %collective-permute-done.8.refs_3_), channel_id=1, source_target_pairs={{0,1},{1,2},{2,3},{3,4},{4,5},{5,6},{6,7},{7,0},{8,9},{9,10},{10,1... | collective-permute-start | bytes 1179656 | tf_op jit(solution)/shard_map/ppermute | solution.py:159
  64.7 50.8 %copy-start.5 = (bf16[32,16,768]{2,1,0:T(8,128)(2,1)}, bf16[32,16,768]{2,1,0:T(8,128)(2,1)S(1)}, u32[]{:S(2)}) copy-start(bf16[32,16,768]{2,1,0:T(8,128)(2,1)S(1)} %constant_dynamic-update-slice_fusion.2.refs_2_) | copy-start | bytes 2359300
  66.0 49.5 %copy-start.4 = (bf16[32,16,768]{2,1,0:T(8,128)(2,1)}, bf16[32,16,768]{2,1,0:T(8,128)(2,1)S(1)}, u32[]{:S(2)}) copy-start(bf16[32,16,768]{2,1,0:T(8,128)(2,1)S(1)} %constant_dynamic-update-slice_fusion.refs_1_) | copy-start | bytes 2359300
  66.0 49.5 %collective-permute-start.4 = (bf16[32,16,768]{2,1,0:T(8,128)(2,1)S(1)}, bf16[32,16,768]{2,1,0:T(8,128)(2,1)}, u32[]{:S(2)}, u32[]{:S(2)}) collective-permute-start(bf16[32,16,768]{2,1,0:T(8,128)(2,1)S(1)} %constant_dynamic-update-slice_fusion.refs_1_), channel_id=1, source_target_pairs={{0,1},{1,2},{2,3},{3,4},{4,5},{5,6},{6,7},{7,0},{8,9},{9,10},{10,1... | collective-permute-start | bytes 2359304 | tf_op jit(solution)/shard_map/ppermute | solution.py:159
  66.2 49.3 %collective-permute-start.5 = (bf16[32,16,768]{2,1,0:T(8,128)(2,1)S(1)}, bf16[32,16,768]{2,1,0:T(8,128)(2,1)}, u32[]{:S(2)}, u32[]{:S(2)}) collective-permute-start(bf16[32,16,768]{2,1,0:T(8,128)(2,1)S(1)} %constant_dynamic-update-slice_fusion.2.refs_2_), channel_id=1, source_target_pairs={{1,0},{2,1},{3,2},{4,3},{5,4},{6,5},{7,6},{0,7},{9,8},{10,9},{11,1... | collective-permute-start | bytes 2359304 | tf_op jit(solution)/shard_map/ppermute | solution.py:159
  70.9 25.3 %collective-permute-start.11 = (bf16[16,16,768]{2,1,0:T(8,128)(2,1)S(1)}, bf16[16,16,768]{2,1,0:T(8,128)(2,1)S(1)}, u32[]{:S(2)}, u32[]{:S(2)}) collective-permute-start(bf16[16,16,768]{2,1,0:T(8,128)(2,1)S(1)} %collective-permute-done.9.refs_4_), channel_id=1, source_target_pairs={{1,0},{2,1},{3,2},{4,3},{5,4},{6,5},{7,6},{0,7},{9,8},{10,9},{11,1... | collective-permute-start | bytes 1179656 | tf_op jit(solution)/shard_map/ppermute | solution.py:159
  74.3 30.3 %collective-permute-start.17 = (bf16[16,16,768]{2,1,0:T(8,128)(2,1)S(1)}, bf16[16,16,768]{2,1,0:T(8,128)(2,1)S(1)}, u32[]{:S(2)}, u32[]{:S(2)}) collective-permute-start(bf16[16,16,768]{2,1,0:T(8,128)(2,1)S(1)} %collective-permute-done.15.refs_11_), channel_id=1, source_target_pairs={{1,0},{2,1},{3,2},{4,3},{5,4},{6,5},{7,6},{0,7},{9,8},{10,9},{11,1... | collective-permute-start | bytes 1179656 | tf_op jit(solution)/shard_map/ppermute | solution.py:159
  80.4 27.6 %collective-permute-start.16 = (bf16[16,16,768]{2,1,0:T(8,128)(2,1)S(1)}, bf16[16,16,768]{2,1,0:T(8,128)(2,1)S(1)}, u32[]{:S(2)}, u32[]{:S(2)}) collective-permute-start(bf16[16,16,768]{2,1,0:T(8,128)(2,1)S(1)} %collective-permute-done.14.refs_10_), channel_id=1, source_target_pairs={{0,1},{1,2},{2,3},{3,4},{4,5},{5,6},{6,7},{7,0},{8,9},{9,10},{10,1... | collective-permute-start | bytes 1179656 | tf_op jit(solution)/shard_map/ppermute | solution.py:159
  96.2 19.4 %collective-permute-start.18 = (bf16[16,16,768]{2,1,0:T(8,128)(2,1)S(1)}, bf16[16,16,768]{2,1,0:T(8,128)(2,1)S(1)}, u32[]{:S(2)}, u32[]{:S(2)}) collective-permute-start(bf16[16,16,768]{2,1,0:T(8,128)(2,1)S(1)} %collective-permute-done.10.refs_5_), channel_id=1, source_target_pairs={{0,1},{1,2},{2,3},{3,4},{4,5},{5,6},{6,7},{7,0},{8,9},{9,10},{10,1... | collective-permute-start | bytes 1179656 | tf_op jit(solution)/shard_map/ppermute | solution.py:192
  104.6 11.0 %collective-permute-start.19 = (bf16[16,16,768]{2,1,0:T(8,128)(2,1)S(1)}, bf16[16,16,768]{2,1,0:T(8,128)(2,1)}, u32[]{:S(2)}, u32[]{:S(2)}) collective-permute-start(bf16[16,16,768]{2,1,0:T(8,128)(2,1)S(1)} %collective-permute-done.17.refs_13_), channel_id=1, source_target_pairs={{1,0},{2,1},{3,2},{4,3},{5,4},{6,5},{7,6},{0,7},{9,8},{10,9},{11,1... | collective-permute-start | bytes 1179656 | tf_op jit(solution)/shard_map/ppermute | solution.py:192
  115.6 18.3 %collective-permute-start.20 = (bf16[32,16,768]{2,1,0:T(8,128)(2,1)}, bf16[32,16,768]{2,1,0:T(8,128)(2,1)S(1)}, u32[]{:S(2)}, u32[]{:S(2)}) collective-permute-start(bf16[32,16,768]{2,1,0:T(8,128)(2,1)} %collective-permute-done.4.refs_3_), channel_id=1, source_target_pairs={{0,1},{1,2},{2,3},{3,4},{4,5},{5,6},{6,7},{7,0},{8,9},{9,10},{10,1... | collective-permute-start | bytes 2359304 | tf_op jit(solution)/shard_map/ppermute | solution.py:159
  115.6 18.2 %collective-permute-start.21 = (bf16[32,16,768]{2,1,0:T(8,128)(2,1)}, bf16[32,16,768]{2,1,0:T(8,128)(2,1)S(1)}, u32[]{:S(2)}, u32[]{:S(2)}) collective-permute-start(bf16[32,16,768]{2,1,0:T(8,128)(2,1)} %collective-permute-done.5.refs_4_), channel_id=1, source_target_pairs={{1,0},{2,1},{3,2},{4,3},{5,4},{6,5},{7,6},{0,7},{9,8},{10,9},{11,1... | collective-permute-start | bytes 2359304 | tf_op jit(solution)/shard_map/ppermute | solution.py:159
  122.6 23.9 %all-to-all-start.1 = ((bf16[32,16,768]{2,1,0:T(8,128)(2,1)}), bf16[32,16,768]{2,1,0:T(8,128)(2,1)S(1)}, u32[]{:S(2)}, u32[]{:S(2)}) async-start(bf16[32,16,768]{2,1,0:T(8,128)(2,1)} %shard_map.94), calls=%async_computation.1 | async-start | bytes 1572864 | tf_op jit(solution)/shard_map/all_to_all | solution.py:214
  133.9 12.6 %collective-permute-start.22 = (bf16[16,16,768]{2,1,0:T(8,128)(2,1)S(1)}, bf16[16,16,768]{2,1,0:T(8,128)(2,1)S(1)}, u32[]{:S(2)}, u32[]{:S(2)}) collective-permute-start(bf16[16,16,768]{2,1,0:T(8,128)(2,1)S(1)} %slice.22), channel_id=1, source_target_pairs={{0,1},{1,2},{2,3},{3,4},{4,5},{5,6},{6,7},{7,0},{8,9},{9,10},{10,1... | collective-permute-start | bytes 1179656 | tf_op jit(solution)/shard_map/ppermute | solution.py:159
  134.0 12.5 %collective-permute-start.23 = (bf16[16,16,768]{2,1,0:T(8,128)(2,1)S(1)}, bf16[16,16,768]{2,1,0:T(8,128)(2,1)}, u32[]{:S(2)}, u32[]{:S(2)}) collective-permute-start(bf16[16,16,768]{2,1,0:T(8,128)(2,1)S(1)} %slice.23), channel_id=1, source_target_pairs={{1,0},{2,1},{3,2},{4,3},{5,4},{6,5},{7,6},{0,7},{9,8},{10,9},{11,1... | collective-permute-start | bytes 1179656 | tf_op jit(solution)/shard_map/ppermute | solution.py:159
  (19 other events, 287.5 us)

commit v4 on v3

--- a/solution.py
+++ b/solution.py
@@ -40,10 +40,12 @@
     copy.wait()
 
 
-def pack_kernel(blocks, target, coef, amp, items):
+def pack_kernel(blocks, target, coef, amp, items, part_a, part_b):
     count, rows, width = amp.shape
     ch_dev, nb_tile = target.shape
     factor = coef[...].astype(F32)
+    part_a[...] = amp[: count // 2]
+    part_b[...] = amp[count // 2 :]
     for b in range(count):
         ch, j = divmod(b, nb_tile)
         to = lax.div(target[ch, j], ch_dev * blocks)
@@ -166,17 +168,16 @@
     block_type = jax.ShapeDtypeStruct((count, rows, width), BF16)
     part_type = jax.ShapeDtypeStruct((ch_dev, tile_rows, width), F32)
     half = count // ch_dev
-    amp_a, amp_b = own_rows[:half], own_rows[half:]
+    half_type = jax.ShapeDtypeStruct((half, rows, width), BF16)
+    items, amp_a, amp_b = call(
+        functools.partial(pack_kernel, blocks),
+        (jax.ShapeDtypeStruct((count, rows, width + META), BF16), half_type, half_type),
+        (coef, own_rows),
+        (target,),
+        moved=6 * 2**20,
+    )
     a1, b1 = both(amp_a, amp_a), both(amp_b, amp_b)
     amp1 = tuple(jnp.concatenate(x, axis=0) for x in zip(a1, b1))
-    items = call(
-        functools.partial(pack_kernel, blocks),
-        jax.ShapeDtypeStruct((count, rows, width + META), BF16),
-        (coef, own_rows),
-        (target,),
-        moved=4 * 2**20,
-    )
-    half_type = jax.ShapeDtypeStruct((count // ch_dev, rows, width), BF16)
     far_a, far_b, homes = call(
         functools.partial(settle_kernel, blocks),
         (half_type, half_type, jax.ShapeDtypeStruct((8, META), I32)),
@@ -201,7 +202,8 @@
             moved=12 * 2**20,
         )
 
-    cycle_most = most((far_a, *fa1, *fa2, *fa3, far_b, *fb1, *fb2, *fb3), w_ph)
+    e_col, e_row = e_part[:, :, None], e_hole[:, None, :]
+    cycle_most = most((far_a, *fa1, *fa2, *fa3, far_b, *fb1, *fb2, *fb3), after(w_ph, e_col, e_row))
     amp3 = both(*after(amp2, cycle_most, far4))
     back = call(
         back_kernel,
@@ -225,8 +227,8 @@
             v_pp,
             returned,
             v_pphh,
-            e_part[:, :, None],
-            e_hole[:, None, :],
+            e_col,
+            e_row,
         ),
         (target, pp_size),
         flops=2 * ch_dev * tile_rows * tile_rows * width,

time: 153 us -> 153 us (level)
    unnamed x52 -> x54, local copies, waits for them, and re-layouts: 4.77 us -> 4.82 us
  transfers between devices with their start and end apart: 26 -> 26, of which waited for: 11 -> 11; matrix products, arithmetic and copies ran while one was open for 4% -> 3% of each run, Pallas kernels for 13% -> 13%
where the time goes in v4:
time: 153 us; the launch traced here: 152 us
  waiting for transfers between devices  61.4 us (40%)
  starting transfers between devices  54.3 us (35%)
  Pallas kernels  27.4 us (18%)
  local copies, waits for them, and re-layouts  8.78 us (6%)
    ppermute x22, waiting for transfers between devices, both(): return (to_right(a), to_left(b))  59.1 us
    ppermute x22, starting transfers between devices, both(): return (to_right(a), to_left(b))  30.7 us
    pallas_call x6, Pallas kernels, call(): pl.pallas_call(kernel, out_shape=outs, in_specs=[smem] * len(scalars) + [...  27.4 us
    all_to_all x1, starting transfers between devices, body(): returned = exchange(back)  9.66 us
    all_to_all x1, starting transfers between devices, body(): exchange(items)  8.59 us
    ppermute x2, starting transfers between devices, body(): far4 = (to_right(fa3[0]), to_left(fb3[1]))  5.36 us
    unnamed x54, local copies, waits for them, and re-layouts  4.82 us
  transfers between devices with their start and end apart: 26, of which 11 were waited for; matrix products, arithmetic and copies ran while one was open for 3% of the time, Pallas kernels for 13%

profile of v4, /device:TPU:1, one launch (start us, length us, event | category | flops | bytes accessed | tf_op | source)
XLA Modules:
  0.0 152.2 jit_solution(4266429480583844365)
XLA Ops:
  0.0 2.6 %shard_map.91 = (bf16[32,16,896]{2,1,0:T(8,128)(2,1)}, bf16[16,16,768]{2,1,0:T(8,128)(2,1)}, bf16[16,16,768]{2,1,0:T(8,128)(2,1)}) custom-call(s32[2,16]{1,0:T(2,128)} %target.3, bf16[2,16]{1,0:T(2,128)(2,1)} %coef.3, bf16[32,16,768]{2,1,0:T(8,128)(2,1)} %bitcast.2), custom_call_target="tpu_custom_call" | custom-call | bytes 6291456 | tf_op jit(solution)/shard_map/pallas_call | solution.py:18
  2.6 8.6 %all-to-all-start = ((bf16[32,16,896]{2,1,0:T(8,128)(2,1)}), bf16[32,16,896]{2,1,0:T(8,128)(2,1)S(1)}, u32[]{:S(2)}, u32[]{:S(2)}) async-start(bf16[32,16,896]{2,1,0:T(8,128)(2,1)} %get-tuple-element.25), calls=%async_computation | async-start | bytes 1835008 | tf_op jit(solution)/shard_map/all_to_all | solution.py:184
  11.2 1.7 %collective-permute-start = (bf16[16,16,768]{2,1,0:T(8,128)(2,1)}, bf16[16,16,768]{2,1,0:T(8,128)(2,1)S(1)}, u32[]{:S(2)}, u32[]{:S(2)}) collective-permute-start(bf16[16,16,768]{2,1,0:T(8,128)(2,1)} %get-tuple-element.21), channel_id=1, source_target_pairs={{0,1},{1,2},{2,3},{3,4},{4,5},{5,6},{6,7},{7,0},{8,9},{9,10},{10,1... | collective-permute-start | bytes 1179656 | tf_op jit(solution)/shard_map/ppermute | solution.py:161
  12.9 4.0 %collective-permute-start.2 = (bf16[16,16,768]{2,1,0:T(8,128)(2,1)}, bf16[16,16,768]{2,1,0:T(8,128)(2,1)}, u32[]{:S(2)}, u32[]{:S(2)}) collective-permute-start(bf16[16,16,768]{2,1,0:T(8,128)(2,1)} %get-tuple-element.21), channel_id=1, source_target_pairs={{1,0},{2,1},{3,2},{4,3},{5,4},{6,5},{7,6},{0,7},{9,8},{10,9},{11,1... | collective-permute-start | bytes 1179656 | tf_op jit(solution)/shard_map/ppermute | solution.py:161
  16.9 2.7 %collective-permute-start.3 = (bf16[16,16,768]{2,1,0:T(8,128)(2,1)}, bf16[16,16,768]{2,1,0:T(8,128)(2,1)}, u32[]{:S(2)}, u32[]{:S(2)}) collective-permute-start(bf16[16,16,768]{2,1,0:T(8,128)(2,1)} %get-tuple-element.22), channel_id=1, source_target_pairs={{1,0},{2,1},{3,2},{4,3},{5,4},{6,5},{7,6},{0,7},{9,8},{10,9},{11,1... | collective-permute-start | bytes 1179656 | tf_op jit(solution)/shard_map/ppermute | solution.py:161
  19.6 6.8 %collective-permute-done = bf16[16,16,768]{2,1,0:T(8,128)(2,1)S(1)} collective-permute-done((bf16[16,16,768]{2,1,0:T(8,128)(2,1)}, bf16[16,16,768]{2,1,0:T(8,128)(2,1)S(1)}, u32[]{:S(2)}, u32[]{:S(2)}) %collective-permute-start) | collective-permute-done | bytes 393248 | tf_op jit(solution)/shard_map/ppermute | solution.py:161
  28.1 2.8 %shard_map.92 = (bf16[16,16,768]{2,1,0:T(8,128)(2,1)}, bf16[16,16,768]{2,1,0:T(8,128)(2,1)}, s32[8,128]{1,0:T(8,128)}) custom-call(bf16[32,16,896]{2,1,0:T(8,128)(2,1)} %copy-done.5), custom_call_target="tpu_custom_call" | custom-call | flops 100000000376832 | bytes 4194304 | tf_op jit(solution)/shard_map/pallas_call | solution.py:18
  31.0 3.9 %collective-permute-done.1 = bf16[16,16,768]{2,1,0:T(8,128)(2,1)} collective-permute-done((bf16[16,16,768]{2,1,0:T(8,128)(2,1)}, bf16[16,16,768]{2,1,0:T(8,128)(2,1)}, u32[]{:S(2)}, u32[]{:S(2)}) %collective-permute-start.1) | collective-permute-done | bytes 393248 | tf_op jit(solution)/shard_map/ppermute | solution.py:161
  34.9 2.7 %collective-permute-start.7 = (bf16[16,16,768]{2,1,0:T(8,128)(2,1)}, bf16[16,16,768]{2,1,0:T(8,128)(2,1)S(1)}, u32[]{:S(2)}, u32[]{:S(2)}) collective-permute-start(bf16[16,16,768]{2,1,0:T(8,128)(2,1)} %get-tuple-element.29.refs_0_), channel_id=1, source_target_pairs={{1,0},{2,1},{3,2},{4,3},{5,4},{6,5},{7,6},{0,7},{9,8},{10,9},{11,1... | collective-permute-start | bytes 1179656 | tf_op jit(solution)/shard_map/ppermute | solution.py:161
  39.0 7.2 %collective-permute-done.6.refs_1_ = bf16[16,16,768]{2,1,0:T(8,128)(2,1)S(1)} collective-permute-done((bf16[16,16,768]{2,1,0:T(8,128)(2,1)}, bf16[16,16,768]{2,1,0:T(8,128)(2,1)S(1)}, u32[]{:S(2)}, u32[]{:S(2)}) %collective-permute-start.6) | collective-permute-done | bytes 393248 | tf_op jit(solution)/shard_map/ppermute | solution.py:161
  46.3 2.7 %collective-permute-start.9 = (bf16[16,16,768]{2,1,0:T(8,128)(2,1)S(1)}, bf16[16,16,768]{2,1,0:T(8,128)(2,1)S(1)}, u32[]{:S(2)}, u32[]{:S(2)}) collective-permute-start(bf16[16,16,768]{2,1,0:T(8,128)(2,1)S(1)} %collective-permute-done.7.refs_2_), channel_id=1, source_target_pairs={{1,0},{2,1},{3,2},{4,3},{5,4},{6,5},{7,6},{0,7},{9,8},{10,9},{11,1... | collective-permute-start | bytes 1179656 | tf_op jit(solution)/shard_map/ppermute | solution.py:161
  48.9 4.8 %collective-permute-done.13.refs_9_ = bf16[16,16,768]{2,1,0:T(8,128)(2,1)S(1)} collective-permute-done((bf16[16,16,768]{2,1,0:T(8,128)(2,1)}, bf16[16,16,768]{2,1,0:T(8,128)(2,1)S(1)}, u32[]{:S(2)}, u32[]{:S(2)}) %collective-permute-start.13) | collective-permute-done | bytes 393248 | tf_op jit(solution)/shard_map/ppermute | solution.py:161
  53.7 3.3 %collective-permute-start.15 = (bf16[16,16,768]{2,1,0:T(8,128)(2,1)S(1)}, bf16[16,16,768]{2,1,0:T(8,128)(2,1)S(1)}, u32[]{:S(2)}, u32[]{:S(2)}) collective-permute-start(bf16[16,16,768]{2,1,0:T(8,128)(2,1)S(1)} %collective-permute-done.13.refs_9_), channel_id=1, source_target_pairs={{1,0},{2,1},{3,2},{4,3},{5,4},{6,5},{7,6},{0,7},{9,8},{10,9},{11,1... | collective-permute-start | bytes 1179656 | tf_op jit(solution)/shard_map/ppermute | solution.py:161
  58.2 4.8 %collective-permute-done.8.refs_3_ = bf16[16,16,768]{2,1,0:T(8,128)(2,1)S(1)} collective-permute-done((bf16[16,16,768]{2,1,0:T(8,128)(2,1)S(1)}, bf16[16,16,768]{2,1,0:T(8,128)(2,1)S(1)}, u32[]{:S(2)}, u32[]{:S(2)}) %collective-permute-start.8) | collective-permute-done | bytes 393248 | tf_op jit(solution)/shard_map/ppermute | solution.py:161
  64.3 1.3 constant_dynamic-update-slice_fusion.refs_1_
  65.9 2.6 %collective-permute-start.5 = (bf16[32,16,768]{2,1,0:T(8,128)(2,1)S(1)}, bf16[32,16,768]{2,1,0:T(8,128)(2,1)}, u32[]{:S(2)}, u32[]{:S(2)}) collective-permute-start(bf16[32,16,768]{2,1,0:T(8,128)(2,1)S(1)} %constant_dynamic-update-slice_fusion.2.refs_2_), channel_id=1, source_target_pairs={{1,0},{2,1},{3,2},{4,3},{5,4},{6,5},{7,6},{0,7},{9,8},{10,9},{11,1... | collective-permute-start | bytes 2359304 | tf_op jit(solution)/shard_map/ppermute | solution.py:161
  68.5 2.0 %collective-permute-done.15.refs_11_ = bf16[16,16,768]{2,1,0:T(8,128)(2,1)S(1)} collective-permute-done((bf16[16,16,768]{2,1,0:T(8,128)(2,1)S(1)}, bf16[16,16,768]{2,1,0:T(8,128)(2,1)S(1)}, u32[]{:S(2)}, u32[]{:S(2)}) %collective-permute-start.15) | collective-permute-done | bytes 393248 | tf_op jit(solution)/shard_map/ppermute | solution.py:161
  70.5 3.4 %collective-permute-start.11 = (bf16[16,16,768]{2,1,0:T(8,128)(2,1)S(1)}, bf16[16,16,768]{2,1,0:T(8,128)(2,1)S(1)}, u32[]{:S(2)}, u32[]{:S(2)}) collective-permute-start(bf16[16,16,768]{2,1,0:T(8,128)(2,1)S(1)} %collective-permute-done.9.refs_4_), channel_id=1, source_target_pairs={{1,0},{2,1},{3,2},{4,3},{5,4},{6,5},{7,6},{0,7},{9,8},{10,9},{11,1... | collective-permute-start | bytes 1179656 | tf_op jit(solution)/shard_map/ppermute | solution.py:161
  74.0 6.0 %collective-permute-done.10.refs_5_ = bf16[16,16,768]{2,1,0:T(8,128)(2,1)S(1)} collective-permute-done((bf16[16,16,768]{2,1,0:T(8,128)(2,1)S(1)}, bf16[16,16,768]{2,1,0:T(8,128)(2,1)S(1)}, u32[]{:S(2)}, u32[]{:S(2)}) %collective-permute-start.10) | collective-permute-done | bytes 393248 | tf_op jit(solution)/shard_map/ppermute | solution.py:161
  79.9 15.8 %collective-permute-done.11.refs_6_ = bf16[16,16,768]{2,1,0:T(8,128)(2,1)S(1)} collective-permute-done((bf16[16,16,768]{2,1,0:T(8,128)(2,1)S(1)}, bf16[16,16,768]{2,1,0:T(8,128)(2,1)S(1)}, u32[]{:S(2)}, u32[]{:S(2)}) %collective-permute-start.11) | collective-permute-done | bytes 393248 | tf_op jit(solution)/shard_map/ppermute | solution.py:161
  95.7 2.0 %collective-permute-start.18 = (bf16[16,16,768]{2,1,0:T(8,128)(2,1)S(1)}, bf16[16,16,768]{2,1,0:T(8,128)(2,1)S(1)}, u32[]{:S(2)}, u32[]{:S(2)}) collective-permute-start(bf16[16,16,768]{2,1,0:T(8,128)(2,1)S(1)} %collective-permute-done.10.refs_5_), channel_id=1, source_target_pairs={{0,1},{1,2},{2,3},{3,4},{4,5},{5,6},{6,7},{7,0},{8,9},{9,10},{10,1... | collective-permute-start | bytes 1179656 | tf_op jit(solution)/shard_map/ppermute | solution.py:193
  97.7 6.5 %collective-permute-done.17.refs_13_ = bf16[16,16,768]{2,1,0:T(8,128)(2,1)S(1)} collective-permute-done((bf16[16,16,768]{2,1,0:T(8,128)(2,1)S(1)}, bf16[16,16,768]{2,1,0:T(8,128)(2,1)S(1)}, u32[]{:S(2)}, u32[]{:S(2)}) %collective-permute-start.17) | collective-permute-done | bytes 393248 | tf_op jit(solution)/shard_map/ppermute | solution.py:161
  104.2 3.4 %collective-permute-start.19 = (bf16[16,16,768]{2,1,0:T(8,128)(2,1)S(1)}, bf16[16,16,768]{2,1,0:T(8,128)(2,1)S(1)}, u32[]{:S(2)}, u32[]{:S(2)}) collective-permute-start(bf16[16,16,768]{2,1,0:T(8,128)(2,1)S(1)} %collective-permute-done.17.refs_13_), channel_id=1, source_target_pairs={{1,0},{2,1},{3,2},{4,3},{5,4},{6,5},{7,6},{0,7},{9,8},{10,9},{11,1... | collective-permute-start | bytes 1179656 | tf_op jit(solution)/shard_map/ppermute | solution.py:193
  109.1 6.6 %shard_map.93.part = f32[2,256,768]{2,1,0:T(8,128)} custom-call(bf16[16,16,768]{2,1,0:T(8,128)(2,1)} %get-tuple-element.29.refs_0_, bf16[16,16,768]{2,1,0:T(8,128)(2,1)} %copy-done.7, bf16[16,16,768]{2,1,0:T(8,128)(2,1)} %copy-done.8, bf16[16,16,768]{2,1,0:T(8,128)(2,1)} %copy-done.11, bf16[16,16,768]{2,1,0:T(8,128)(2,1)} %copy-done.12, ...), custom_call_target="tpu_custom_call" | custom-call | flops 1610612736 | bytes 12582912 | tf_op jit(solution)/shard_map/pallas_call | solution.py:18
  115.9 2.7 %collective-permute-start.21 = (bf16[32,16,768]{2,1,0:T(8,128)(2,1)}, bf16[32,16,768]{2,1,0:T(8,128)(2,1)S(1)}, u32[]{:S(2)}, u32[]{:S(2)}) collective-permute-start(bf16[32,16,768]{2,1,0:T(8,128)(2,1)} %collective-permute-done.5.refs_4_), channel_id=1, source_target_pairs={{1,0},{2,1},{3,2},{4,3},{5,4},{6,5},{7,6},{0,7},{9,8},{10,9},{11,1... | collective-permute-start | bytes 2359304 | tf_op jit(solution)/shard_map/ppermute | solution.py:161
  118.6 4.3 %shard_map.94 = bf16[32,16,768]{2,1,0:T(8,128)(2,1)} custom-call(s32[8,128]{1,0:T(8,128)} %get-tuple-element.34.homes, bf16[16,16,768]{2,1,0:T(8,128)(2,1)} %copy-done.19, bf16[16,16,768]{2,1,0:T(8,128)(2,1)} %copy-done.20, f32[2,256,768]{2,1,0:T(8,128)} %shard_map.93.part, bf16[2,256,2048]{2,1,0:T(8,128)(2,1)} %w_ph.1), custom_call_target="tpu_custom_call" | custom-call | flops 201326592 | bytes 6291456 | tf_op jit(solution)/shard_map/pallas_call | solution.py:18
  122.9 9.7 %all-to-all-start.1 = ((bf16[32,16,768]{2,1,0:T(8,128)(2,1)}), bf16[32,16,768]{2,1,0:T(8,128)(2,1)S(1)}, u32[]{:S(2)}, u32[]{:S(2)}) async-start(bf16[32,16,768]{2,1,0:T(8,128)(2,1)} %shard_map.94), calls=%async_computation.1 | async-start | bytes 1572864 | tf_op jit(solution)/shard_map/all_to_all | solution.py:216
  132.5 1.4 collective-permute-done.20.refs_5_
  134.1 3.0 %collective-permute-start.23 = (bf16[16,16,768]{2,1,0:T(8,128)(2,1)S(1)}, bf16[16,16,768]{2,1,0:T(8,128)(2,1)}, u32[]{:S(2)}, u32[]{:S(2)}) collective-permute-start(bf16[16,16,768]{2,1,0:T(8,128)(2,1)S(1)} %slice.7), channel_id=1, source_target_pairs={{1,0},{2,1},{3,2},{4,3},{5,4},{6,5},{7,6},{0,7},{9,8},{10,9},{11,1... | collective-permute-start | bytes 1179656 | tf_op jit(solution)/shard_map/ppermute | solution.py:161
  137.9 6.6 %shard_map.95.part = f32[2,256,768]{2,1,0:T(8,128)} custom-call(bf16[32,16,768]{2,1,0:T(8,128)(2,1)} %bitcast.3, bf16[32,16,768]{2,1,0:T(8,128)(2,1)} %copy-done.3, bf16[32,16,768]{2,1,0:T(8,128)(2,1)} %copy-done.4, bf16[32,16,768]{2,1,0:T(8,128)(2,1)} %copy-done.6, bf16[32,16,768]{2,1,0:T(8,128)(2,1)} %collective-permute-done.5.refs_4_, ...), custom_call_target="tpu_custom_call" | custom-call | flops 1610612736 | bytes 12582912 | tf_op jit(solution)/shard_map/pallas_call | solution.py:18
  144.5 2.2 %all-to-all-done.1.back = bf16[32,16,768]{2,1,0:T(8,128)(2,1)S(1)} async-done(((bf16[32,16,768]{2,1,0:T(8,128)(2,1)}), bf16[32,16,768]{2,1,0:T(8,128)(2,1)S(1)}, u32[]{:S(2)}, u32[]{:S(2)}) %all-to-all-start.1) | async-done | bytes 786464 | tf_op jit(solution)/shard_map/all_to_all | solution.py:216
  147.8 4.5 %shard_map.96 = bf16[2,256,768]{2,1,0:T(8,128)(2,1)} custom-call(s32[2,16]{1,0:T(2,128)} %target.3, s32[2]{0:T(128)} %live.1, bf16[2,16]{1,0:T(2,128)(2,1)} %coef.3, bf16[16,16,768]{2,1,0:T(8,128)(2,1)} %copy-done.23, bf16[16,16,768]{2,1,0:T(8,128)(2,1)} %collective-permute-done.23.half_b, f32[2,256,768]{2,1,0:T(8,128)} %shard_map.95.part, ...), custom_call_target="tpu_custom_call" | custom-call | flops 201326592 | bytes 6291456 | tf_op jit(solution)/shard_map/pallas_call | solution.py:18
  (86 shorter events, 9.5 us)
Async XLA Ops:
  2.6 24.6 %all-to-all-start = ((bf16[32,16,896]{2,1,0:T(8,128)(2,1)}), bf16[32,16,896]{2,1,0:T(8,128)(2,1)S(1)}, u32[]{:S(2)}, u32[]{:S(2)}) async-start(bf16[32,16,896]{2,1,0:T(8,128)(2,1)} %get-tuple-element.25), calls=%async_computation | async-start | bytes 1835008 | tf_op jit(solution)/shard_map/all_to_all | solution.py:184
  11.2 15.2 %collective-permute-start = (bf16[16,16,768]{2,1,0:T(8,128)(2,1)}, bf16[16,16,768]{2,1,0:T(8,128)(2,1)S(1)}, u32[]{:S(2)}, u32[]{:S(2)}) collective-permute-start(bf16[16,16,768]{2,1,0:T(8,128)(2,1)} %get-tuple-element.21), channel_id=1, source_target_pairs={{0,1},{1,2},{2,3},{3,4},{4,5},{5,6},{6,7},{7,0},{8,9},{9,10},{10,1... | collective-permute-start | bytes 1179656 | tf_op jit(solution)/shard_map/ppermute | solution.py:161
  12.9 14.3 %collective-permute-start.2 = (bf16[16,16,768]{2,1,0:T(8,128)(2,1)}, bf16[16,16,768]{2,1,0:T(8,128)(2,1)}, u32[]{:S(2)}, u32[]{:S(2)}) collective-permute-start(bf16[16,16,768]{2,1,0:T(8,128)(2,1)} %get-tuple-element.21), channel_id=1, source_target_pairs={{1,0},{2,1},{3,2},{4,3},{5,4},{6,5},{7,6},{0,7},{9,8},{10,9},{11,1... | collective-permute-start | bytes 1179656 | tf_op jit(solution)/shard_map/ppermute | solution.py:161
  16.9 18.0 %collective-permute-start.1 = (bf16[16,16,768]{2,1,0:T(8,128)(2,1)}, bf16[16,16,768]{2,1,0:T(8,128)(2,1)}, u32[]{:S(2)}, u32[]{:S(2)}) collective-permute-start(bf16[16,16,768]{2,1,0:T(8,128)(2,1)} %get-tuple-element.22), channel_id=1, source_target_pairs={{0,1},{1,2},{2,3},{3,4},{4,5},{5,6},{6,7},{7,0},{8,9},{9,10},{10,1... | collective-permute-start | bytes 1179656 | tf_op jit(solution)/shard_map/ppermute | solution.py:161
  16.9 18.0 %collective-permute-start.3 = (bf16[16,16,768]{2,1,0:T(8,128)(2,1)}, bf16[16,16,768]{2,1,0:T(8,128)(2,1)}, u32[]{:S(2)}, u32[]{:S(2)}) collective-permute-start(bf16[16,16,768]{2,1,0:T(8,128)(2,1)} %get-tuple-element.22), channel_id=1, source_target_pairs={{1,0},{2,1},{3,2},{4,3},{5,4},{6,5},{7,6},{0,7},{9,8},{10,9},{11,1... | collective-permute-start | bytes 1179656 | tf_op jit(solution)/shard_map/ppermute | solution.py:161
  31.0 76.6 %copy-start.24 = (f32[2,768]{1,0:T(2,128)S(1)}, f32[2,768]{1,0:T(2,128)}, u32[]{:S(2)}) copy-start(f32[2,768]{1,0:T(2,128)} %param.17) | copy-start | bytes 18436
  34.9 11.3 %collective-permute-start.6 = (bf16[16,16,768]{2,1,0:T(8,128)(2,1)}, bf16[16,16,768]{2,1,0:T(8,128)(2,1)S(1)}, u32[]{:S(2)}, u32[]{:S(2)}) collective-permute-start(bf16[16,16,768]{2,1,0:T(8,128)(2,1)} %get-tuple-element.29.refs_0_), channel_id=1, source_target_pairs={{0,1},{1,2},{2,3},{3,4},{4,5},{5,6},{6,7},{7,0},{8,9},{9,10},{10,1... | collective-permute-start | bytes 1179656 | tf_op jit(solution)/shard_map/ppermute | solution.py:161
  34.9 11.3 %collective-permute-start.7 = (bf16[16,16,768]{2,1,0:T(8,128)(2,1)}, bf16[16,16,768]{2,1,0:T(8,128)(2,1)S(1)}, u32[]{:S(2)}, u32[]{:S(2)}) collective-permute-start(bf16[16,16,768]{2,1,0:T(8,128)(2,1)} %get-tuple-element.29.refs_0_), channel_id=1, source_target_pairs={{1,0},{2,1},{3,2},{4,3},{5,4},{6,5},{7,6},{0,7},{9,8},{10,9},{11,1... | collective-permute-start | bytes 1179656 | tf_op jit(solution)/shard_map/ppermute | solution.py:161
  37.6 16.1 %collective-permute-start.13 = (bf16[16,16,768]{2,1,0:T(8,128)(2,1)}, bf16[16,16,768]{2,1,0:T(8,128)(2,1)S(1)}, u32[]{:S(2)}, u32[]{:S(2)}) collective-permute-start(bf16[16,16,768]{2,1,0:T(8,128)(2,1)} %get-tuple-element.30.refs_7_), channel_id=1, source_target_pairs={{1,0},{2,1},{3,2},{4,3},{5,4},{6,5},{7,6},{0,7},{9,8},{10,9},{11,1... | collective-permute-start | bytes 1179656 | tf_op jit(solution)/shard_map/ppermute | solution.py:161
  38.8 18.2 %collective-permute-start.12 = (bf16[16,16,768]{2,1,0:T(8,128)(2,1)}, bf16[16,16,768]{2,1,0:T(8,128)(2,1)S(1)}, u32[]{:S(2)}, u32[]{:S(2)}) collective-permute-start(bf16[16,16,768]{2,1,0:T(8,128)(2,1)} %get-tuple-element.30.refs_7_), channel_id=1, source_target_pairs={{0,1},{1,2},{2,3},{3,4},{4,5},{5,6},{6,7},{7,0},{8,9},{9,10},{10,1... | collective-permute-start | bytes 1179656 | tf_op jit(solution)/shard_map/ppermute | solution.py:161
  46.2 61.9 %copy-start.7 = (bf16[16,16,768]{2,1,0:T(8,128)(2,1)}, bf16[16,16,768]{2,1,0:T(8,128)(2,1)S(1)}, u32[]{:S(2)}) copy-start(bf16[16,16,768]{2,1,0:T(8,128)(2,1)S(1)} %collective-permute-done.6.refs_1_) | copy-start | bytes 1179652
  46.2 16.9 %collective-permute-start.8 = (bf16[16,16,768]{2,1,0:T(8,128)(2,1)S(1)}, bf16[16,16,768]{2,1,0:T(8,128)(2,1)S(1)}, u32[]{:S(2)}, u32[]{:S(2)}) collective-permute-start(bf16[16,16,768]{2,1,0:T(8,128)(2,1)S(1)} %collective-permute-done.6.refs_1_), channel_id=1, source_target_pairs={{0,1},{1,2},{2,3},{3,4},{4,5},{5,6},{6,7},{7,0},{8,9},{9,10},{10,1... | collective-permute-start | bytes 1179656 | tf_op jit(solution)/shard_map/ppermute | solution.py:161
  46.2 61.9 %copy-start.8 = (bf16[16,16,768]{2,1,0:T(8,128)(2,1)}, bf16[16,16,768]{2,1,0:T(8,128)(2,1)S(1)}, u32[]{:S(2)}) copy-start(bf16[16,16,768]{2,1,0:T(8,128)(2,1)S(1)} %collective-permute-done.7.refs_2_) | copy-start | bytes 1179652
  46.3 19.6 %collective-permute-start.9 = (bf16[16,16,768]{2,1,0:T(8,128)(2,1)S(1)}, bf16[16,16,768]{2,1,0:T(8,128)(2,1)S(1)}, u32[]{:S(2)}, u32[]{:S(2)}) collective-permute-start(bf16[16,16,768]{2,1,0:T(8,128)(2,1)S(1)} %collective-permute-done.7.refs_2_), channel_id=1, source_target_pairs={{1,0},{2,1},{3,2},{4,3},{5,4},{6,5},{7,6},{0,7},{9,8},{10,9},{11,1... | collective-permute-start | bytes 1179656 | tf_op jit(solution)/shard_map/ppermute | solution.py:161
  53.7 54.5 %copy-start.9 = (bf16[16,16,768]{2,1,0:T(8,128)(2,1)}, bf16[16,16,768]{2,1,0:T(8,128)(2,1)S(1)}, u32[]{:S(2)}) copy-start(bf16[16,16,768]{2,1,0:T(8,128)(2,1)S(1)} %collective-permute-done.13.refs_9_) | copy-start | bytes 1179652
  53.7 16.7 %collective-permute-start.15 = (bf16[16,16,768]{2,1,0:T(8,128)(2,1)S(1)}, bf16[16,16,768]{2,1,0:T(8,128)(2,1)S(1)}, u32[]{:S(2)}, u32[]{:S(2)}) collective-permute-start(bf16[16,16,768]{2,1,0:T(8,128)(2,1)S(1)} %collective-permute-done.13.refs_9_), channel_id=1, source_target_pairs={{1,0},{2,1},{3,2},{4,3},{5,4},{6,5},{7,6},{0,7},{9,8},{10,9},{11,1... | collective-permute-start | bytes 1179656 | tf_op jit(solution)/shard_map/ppermute | solution.py:161
  57.0 51.2 %copy-start.10 = (bf16[16,16,768]{2,1,0:T(8,128)(2,1)}, bf16[16,16,768]{2,1,0:T(8,128)(2,1)S(1)}, u32[]{:S(2)}) copy-start(bf16[16,16,768]{2,1,0:T(8,128)(2,1)S(1)} %collective-permute-done.12.refs_8_) | copy-start | bytes 1179652
  57.0 16.9 %collective-permute-start.14 = (bf16[16,16,768]{2,1,0:T(8,128)(2,1)S(1)}, bf16[16,16,768]{2,1,0:T(8,128)(2,1)S(1)}, u32[]{:S(2)}, u32[]{:S(2)}) collective-permute-start(bf16[16,16,768]{2,1,0:T(8,128)(2,1)S(1)} %collective-permute-done.12.refs_8_), channel_id=1, source_target_pairs={{0,1},{1,2},{2,3},{3,4},{4,5},{5,6},{6,7},{7,0},{8,9},{9,10},{10,1... | collective-permute-start | bytes 1179656 | tf_op jit(solution)/shard_map/ppermute | solution.py:161
  63.1 16.9 %collective-permute-start.10 = (bf16[16,16,768]{2,1,0:T(8,128)(2,1)S(1)}, bf16[16,16,768]{2,1,0:T(8,128)(2,1)S(1)}, u32[]{:S(2)}, u32[]{:S(2)}) collective-permute-start(bf16[16,16,768]{2,1,0:T(8,128)(2,1)S(1)} %collective-permute-done.8.refs_3_), channel_id=1, source_target_pairs={{0,1},{1,2},{2,3},{3,4},{4,5},{5,6},{6,7},{7,0},{8,9},{9,10},{10,1... | collective-permute-start | bytes 1179656 | tf_op jit(solution)/shard_map/ppermute | solution.py:161
  64.3 51.4 %copy-start.4 = (bf16[32,16,768]{2,1,0:T(8,128)(2,1)}, bf16[32,16,768]{2,1,0:T(8,128)(2,1)S(1)}, u32[]{:S(2)}) copy-start(bf16[32,16,768]{2,1,0:T(8,128)(2,1)S(1)} %constant_dynamic-update-slice_fusion.2.refs_2_) | copy-start | bytes 2359300
  65.6 50.1 %collective-permute-start.4 = (bf16[32,16,768]{2,1,0:T(8,128)(2,1)S(1)}, bf16[32,16,768]{2,1,0:T(8,128)(2,1)S(1)}, u32[]{:S(2)}, u32[]{:S(2)}) collective-permute-start(bf16[32,16,768]{2,1,0:T(8,128)(2,1)S(1)} %constant_dynamic-update-slice_fusion.refs_1_), channel_id=1, source_target_pairs={{0,1},{1,2},{2,3},{3,4},{4,5},{5,6},{6,7},{7,0},{8,9},{9,10},{10,1... | collective-permute-start | bytes 2359304 | tf_op jit(solution)/shard_map/ppermute | solution.py:161
  65.9 49.9 %collective-permute-start.5 = (bf16[32,16,768]{2,1,0:T(8,128)(2,1)S(1)}, bf16[32,16,768]{2,1,0:T(8,128)(2,1)}, u32[]{:S(2)}, u32[]{:S(2)}) collective-permute-start(bf16[32,16,768]{2,1,0:T(8,128)(2,1)S(1)} %constant_dynamic-update-slice_fusion.2.refs_2_), channel_id=1, source_target_pairs={{1,0},{2,1},{3,2},{4,3},{5,4},{6,5},{7,6},{0,7},{9,8},{10,9},{11,1... | collective-permute-start | bytes 2359304 | tf_op jit(solution)/shard_map/ppermute | solution.py:161
  70.5 25.3 %collective-permute-start.11 = (bf16[16,16,768]{2,1,0:T(8,128)(2,1)S(1)}, bf16[16,16,768]{2,1,0:T(8,128)(2,1)S(1)}, u32[]{:S(2)}, u32[]{:S(2)}) collective-permute-start(bf16[16,16,768]{2,1,0:T(8,128)(2,1)S(1)} %collective-permute-done.9.refs_4_), channel_id=1, source_target_pairs={{1,0},{2,1},{3,2},{4,3},{5,4},{6,5},{7,6},{0,7},{9,8},{10,9},{11,1... | collective-permute-start | bytes 1179656 | tf_op jit(solution)/shard_map/ppermute | solution.py:161
  73.9 30.3 %collective-permute-start.17 = (bf16[16,16,768]{2,1,0:T(8,128)(2,1)S(1)}, bf16[16,16,768]{2,1,0:T(8,128)(2,1)S(1)}, u32[]{:S(2)}, u32[]{:S(2)}) collective-permute-start(bf16[16,16,768]{2,1,0:T(8,128)(2,1)S(1)} %collective-permute-done.15.refs_11_), channel_id=1, source_target_pairs={{1,0},{2,1},{3,2},{4,3},{5,4},{6,5},{7,6},{0,7},{9,8},{10,9},{11,1... | collective-permute-start | bytes 1179656 | tf_op jit(solution)/shard_map/ppermute | solution.py:161
  79.9 28.2 %collective-permute-start.16 = (bf16[16,16,768]{2,1,0:T(8,128)(2,1)S(1)}, bf16[16,16,768]{2,1,0:T(8,128)(2,1)S(1)}, u32[]{:S(2)}, u32[]{:S(2)}) collective-permute-start(bf16[16,16,768]{2,1,0:T(8,128)(2,1)S(1)} %collective-permute-done.14.refs_10_), channel_id=1, source_target_pairs={{0,1},{1,2},{2,3},{3,4},{4,5},{5,6},{6,7},{7,0},{8,9},{9,10},{10,1... | collective-permute-start | bytes 1179656 | tf_op jit(solution)/shard_map/ppermute | solution.py:161
  95.7 20.0 %collective-permute-start.18 = (bf16[16,16,768]{2,1,0:T(8,128)(2,1)S(1)}, bf16[16,16,768]{2,1,0:T(8,128)(2,1)S(1)}, u32[]{:S(2)}, u32[]{:S(2)}) collective-permute-start(bf16[16,16,768]{2,1,0:T(8,128)(2,1)S(1)} %collective-permute-done.10.refs_5_), channel_id=1, source_target_pairs={{0,1},{1,2},{2,3},{3,4},{4,5},{5,6},{6,7},{7,0},{8,9},{9,10},{10,1... | collective-permute-start | bytes 1179656 | tf_op jit(solution)/shard_map/ppermute | solution.py:193
  104.2 11.6 %collective-permute-start.19 = (bf16[16,16,768]{2,1,0:T(8,128)(2,1)S(1)}, bf16[16,16,768]{2,1,0:T(8,128)(2,1)S(1)}, u32[]{:S(2)}, u32[]{:S(2)}) collective-permute-start(bf16[16,16,768]{2,1,0:T(8,128)(2,1)S(1)} %collective-permute-done.17.refs_13_), channel_id=1, source_target_pairs={{1,0},{2,1},{3,2},{4,3},{5,4},{6,5},{7,6},{0,7},{9,8},{10,9},{11,1... | collective-permute-start | bytes 1179656 | tf_op jit(solution)/shard_map/ppermute | solution.py:193
  115.8 18.1 %collective-permute-start.20 = (bf16[32,16,768]{2,1,0:T(8,128)(2,1)S(1)}, bf16[32,16,768]{2,1,0:T(8,128)(2,1)S(1)}, u32[]{:S(2)}, u32[]{:S(2)}) collective-permute-start(bf16[32,16,768]{2,1,0:T(8,128)(2,1)S(1)} %collective-permute-done.4.refs_3_), channel_id=1, source_target_pairs={{0,1},{1,2},{2,3},{3,4},{4,5},{5,6},{6,7},{7,0},{8,9},{9,10},{10,1... | collective-permute-start | bytes 2359304 | tf_op jit(solution)/shard_map/ppermute | solution.py:161
  115.9 18.0 %collective-permute-start.21 = (bf16[32,16,768]{2,1,0:T(8,128)(2,1)}, bf16[32,16,768]{2,1,0:T(8,128)(2,1)S(1)}, u32[]{:S(2)}, u32[]{:S(2)}) collective-permute-start(bf16[32,16,768]{2,1,0:T(8,128)(2,1)} %collective-permute-done.5.refs_4_), channel_id=1, source_target_pairs={{1,0},{2,1},{3,2},{4,3},{5,4},{6,5},{7,6},{0,7},{9,8},{10,9},{11,1... | collective-permute-start | bytes 2359304 | tf_op jit(solution)/shard_map/ppermute | solution.py:161
  122.9 23.9 %all-to-all-start.1 = ((bf16[32,16,768]{2,1,0:T(8,128)(2,1)}), bf16[32,16,768]{2,1,0:T(8,128)(2,1)S(1)}, u32[]{:S(2)}, u32[]{:S(2)}) async-start(bf16[32,16,768]{2,1,0:T(8,128)(2,1)} %shard_map.94), calls=%async_computation.1 | async-start | bytes 1572864 | tf_op jit(solution)/shard_map/all_to_all | solution.py:216
  133.9 12.8 %collective-permute-start.22 = (bf16[16,16,768]{2,1,0:T(8,128)(2,1)S(1)}, bf16[16,16,768]{2,1,0:T(8,128)(2,1)S(1)}, u32[]{:S(2)}, u32[]{:S(2)}) collective-permute-start(bf16[16,16,768]{2,1,0:T(8,128)(2,1)S(1)} %slice.6), channel_id=1, source_target_pairs={{0,1},{1,2},{2,3},{3,4},{4,5},{5,6},{6,7},{7,0},{8,9},{9,10},{10,1... | collective-permute-start | bytes 1179656 | tf_op jit(solution)/shard_map/ppermute | solution.py:161
  134.1 12.7 %collective-permute-start.23 = (bf16[16,16,768]{2,1,0:T(8,128)(2,1)S(1)}, bf16[16,16,768]{2,1,0:T(8,128)(2,1)}, u32[]{:S(2)}, u32[]{:S(2)}) collective-permute-start(bf16[16,16,768]{2,1,0:T(8,128)(2,1)S(1)} %slice.7), channel_id=1, source_target_pairs={{1,0},{2,1},{3,2},{4,3},{5,4},{6,5},{7,6},{0,7},{9,8},{10,9},{11,1... | collective-permute-start | bytes 1179656 | tf_op jit(solution)/shard_map/ppermute | solution.py:161
  (20 other events, 324.0 us)
